TPU v7x, 128 devices: a whole 4x4x4 slice. The times are simulated.
128 devices in a mesh: ctx: 32 (over x_hi, z, y), ep: 4 (over x_lo, core).
Axes of the slice: x: 4 (x_hi: 2, x_lo: 2; x = x_hi * 2 + x_lo), y: 4, z: 4, core: 2. Of those that a mesh axis runs over, the one named last changes fastest.
Arguments:
- q_nope: bfloat16 [4096, 8192], P('ctx', 'ep'), may hold values from -6 to 6
- q_rope: bfloat16 [4096, 4096], P('ctx', 'ep'), may hold values from -300 to 300
- latent: bfloat16 [4096, 512], P('ctx'), may hold values from -6 to 6
- k_rope: bfloat16 [4096, 64], P('ctx'), may hold values from -5 to 5
- w_uk: bfloat16 [512, 8192], P(None, 'ep'), may hold values from -0.25 to 0.25
- w_uv: bfloat16 [512, 8192], P(None, 'ep'), may hold values from -0.25 to 0.25
- positions: int32 [4096], replicated, may hold values from 0 to 4095, as said below
- moe_rows: bfloat16 [4096, 7168], P('ctx', 'ep'), may hold values from -6 to 6
- expert_ids: int32 [4096, 8], P('ctx'), may hold values from 0 to 255, all different within a row; in each aligned block of 128 rows (0 to 127, 128 to 255, ...) at most 8 rows name the same one
- expert_weights: float32 [4096, 8], P('ctx'), may hold values from 0.05 to 0.5
- w_gate: bfloat16 [32, 7168, 1024], P('ctx', None, 'ep'), may hold values from -0.0625 to 0.0625
- w_up: bfloat16 [32, 7168, 1024], P('ctx', None, 'ep'), may hold values from -0.0625 to 0.0625
- w_down: bfloat16 [32, 1024, 7168], P('ctx', 'ep'), may hold values from -0.1875 to 0.1875
Outputs:
- attention: bfloat16 [4096, 8192], P('ctx', 'ep')
- moe_out: bfloat16 [4096, 7168], P('ctx', 'ep')
Inputs may be any that keep to these rules, and one draw needn't show every extreme that they name: `expert_ids`: each row names 8 different experts; in each aligned block of 128 rows (the rows of one index of ctx) no expert is named by more than 8 rows. A permutation of the positions; the 128 rows of each index of ctx are two runs of 64 consecutive positions, run j and run 2 * 32 - 1 - j of the prompt for some j.
All inputs are finite; a program needn't handle non-finite values.
Results may differ from a plain program's by a relative error of at most 0.017.
Values may be sent and summed in bfloat16 or wider, within the bound.
A program may use at most 192 MiB of HBM per device.

v0:
```python
import math

import jax
import jax.numpy as jnp
from jax import lax
from jax.sharding import PartitionSpec as P

NOPE = 128
ROPE = 64
VDIM = 128
TOP = 8
CAP = 8


def latent_attention(q_nope, q_rope, latent, k_rope, w_uk, w_uv, positions):
    query_count = q_nope.shape[0]
    head_count = w_uk.shape[1] // NOPE
    context_index = lax.axis_index("ctx")
    query_positions = lax.dynamic_slice_in_dim(positions, context_index * query_count, query_count)
    query_nope = q_nope.reshape(query_count, head_count, NOPE)
    query_rope = q_rope.reshape(query_count, head_count, ROPE)
    score_scale = 1.0 / math.sqrt(NOPE + ROPE)
    block_latent = lax.all_gather(latent, "ctx", axis=0, tiled=True)
    block_rope = lax.all_gather(k_rope, "ctx", axis=0, tiled=True)
    key_count = block_latent.shape[0]
    keys_nope = (
        jnp.dot(block_latent, w_uk, preferred_element_type=jnp.float32)
        .astype(jnp.bfloat16)
        .reshape(key_count, head_count, NOPE)
    )
    block_values = (
        jnp.dot(block_latent, w_uv, preferred_element_type=jnp.float32)
        .astype(jnp.bfloat16)
        .reshape(key_count, head_count, VDIM)
    )
    scores = jnp.einsum("qhd,khd->hqk", query_nope, keys_nope, preferred_element_type=jnp.float32)
    scores = (
        scores
        + jnp.einsum("qhd,kd->hqk", query_rope, block_rope, preferred_element_type=jnp.float32)
    ) * score_scale
    visible = (positions[None, :] <= query_positions[:, None])[None]
    scores = jnp.where(visible, scores, -jnp.inf)
    running_max = jnp.full((head_count, query_count), -1e30, jnp.float32)
    new_max = jnp.maximum(running_max, jnp.max(scores, axis=2))
    weights_exp = jnp.where(visible, jnp.exp(scores - new_max[:, :, None]), 0.0)
    new_total = jnp.sum(weights_exp, axis=2)
    new_sum = jnp.einsum(
        "hqk,khd->hqd",
        weights_exp.astype(jnp.bfloat16),
        block_values,
        preferred_element_type=jnp.float32,
    )
    result = (
        (new_sum / new_total[:, :, None]).transpose(1, 0, 2).reshape(query_count, head_count * VDIM)
    )
    return result.astype(jnp.bfloat16)


def weighted_sum(slot_values, gather_index, weights_used):
    total = jnp.zeros((gather_index.shape[0], slot_values.shape[1]), jnp.float32)
    for choice_slot in range(gather_index.shape[1]):
        total = (
            total
            + slot_values[gather_index[:, choice_slot]] * weights_used[:, choice_slot][:, None]
        )
    return total


def expert_layer(moe_rows, expert_ids, expert_weights, w_gate, w_up, w_down):
    row_count, feature_part = moe_rows.shape
    window = lax.axis_size("ctx")
    flat_experts = expert_ids.reshape(-1)
    in_window = flat_experts < window
    one_hot = (
        (flat_experts[:, None] == jnp.arange(window, dtype=jnp.int32)[None, :]) & in_window[:, None]
    ).astype(jnp.int32)
    earlier = jnp.cumsum(one_hot, axis=0) - one_hot
    rank_in_expert = jnp.sum(earlier * one_hot, axis=1)
    slot_flat = jnp.where(in_window, flat_experts * CAP + rank_in_expert, window * CAP)
    token_index = jnp.repeat(jnp.arange(row_count, dtype=jnp.int32), TOP)
    source_rows = jnp.zeros((window * CAP,), jnp.int32).at[slot_flat].set(token_index, mode="drop")
    filled = (
        jnp.zeros((window * CAP,), jnp.bfloat16)
        .at[slot_flat]
        .set(jnp.ones(slot_flat.shape, jnp.bfloat16), mode="drop")
    )
    outgoing = (moe_rows[source_rows] * filled[:, None]).reshape(window, CAP, feature_part)
    arrived = lax.all_to_all(outgoing, "ctx", split_axis=0, concat_axis=0, tiled=True)
    slot_rows = arrived.reshape(window * CAP, feature_part)
    gate_local = w_gate[0]
    up_local = w_up[0]
    down_local = w_down[0]
    shard_piece = lax.all_gather(slot_rows, "ep", axis=1, tiled=True)
    gate_value = jnp.dot(shard_piece, gate_local, preferred_element_type=jnp.float32)
    up_value = jnp.dot(shard_piece, up_local, preferred_element_type=jnp.float32)
    hidden = (jax.nn.silu(gate_value) * up_value).astype(jnp.bfloat16)
    partial_out = jnp.dot(hidden, down_local, preferred_element_type=jnp.float32)
    weights_used = jnp.where(in_window, expert_weights.reshape(-1), 0.0).reshape(row_count, TOP)
    gather_index = jnp.where(in_window, slot_flat, 0).reshape(row_count, TOP)
    returned = lax.all_to_all(
        partial_out.reshape(window, CAP, partial_out.shape[1]).astype(jnp.bfloat16),
        "ctx",
        split_axis=0,
        concat_axis=0,
        tiled=True,
    ).astype(jnp.float32)
    combined_full = weighted_sum(
        returned.reshape(window * CAP, partial_out.shape[1]), gather_index, weights_used
    )
    combined = lax.psum_scatter(
        combined_full.astype(jnp.bfloat16), "ep", scatter_dimension=1, tiled=True
    )
    return combined


def shards(
    q_nope,
    q_rope,
    latent,
    k_rope,
    w_uk,
    w_uv,
    positions,
    moe_rows,
    expert_ids,
    expert_weights,
    w_gate,
    w_up,
    w_down,
):
    attention = latent_attention(q_nope, q_rope, latent, k_rope, w_uk, w_uv, positions)
    moe_out = expert_layer(moe_rows, expert_ids, expert_weights, w_gate, w_up, w_down)
    return (attention, moe_out)


def solution(mesh):
    return jax.shard_map(
        shards,
        mesh=mesh,
        in_specs=(
            P("ctx", "ep"),
            P("ctx", "ep"),
            P("ctx", None),
            P("ctx", None),
            P(None, "ep"),
            P(None, "ep"),
            P(),
            P("ctx", "ep"),
            P("ctx", None),
            P("ctx", None),
            P("ctx", None, "ep"),
            P("ctx", None, "ep"),
            P("ctx", "ep", None),
        ),
        out_specs=(P("ctx", "ep"), P("ctx", "ep")),
        check_vma=False,
    )
```

profile of v0, /device:TPU:24, one launch (start us, length us, event | category | flops | bytes accessed | tf_op | source)
XLA Modules:
  0.0 404.6 jit_solution(822705460363711060)
XLA Ops:
  7.2 1.0 copy.36
  8.4 9.0 %reduce-window.6 = s32[32,8,128]{2,1,0:T(8,128)S(1)} reduce-window(s32[32,8,128]{2,1,0:T(8,128)S(1)} %fusion.49, s32[]{:T(128)} %constant.18.clone.1), window={size=1x1x128 pad=0_0x0_0x127_0}, to_apply=%region_2.3 | reduce-window | flops 4161536 | bytes 262148 | tf_op jit(solution)/shard_map/reduce-window
  18.1 0.8 copy.42
  19.2 4.3 %scatter_custom_fusion = s32[256]{0:T(256)S(1)} fusion(s32[1024]{0:T(1024)S(1)} %bitcast.96, s32[1024]{0:T(1024)S(1)} %reshape.231, s32[]{:T(128)} %constant.18.clone.1), kind=kCustom, calls=%fused_computation.101 | custom fusion | bytes 1028 | tf_op jit(solution)/shard_map/scatter | solution.py:81
  23.6 7.6 %scatter_custom_fusion.1 = bf16[256]{0:T(256)(128)(2,1)S(1)} fusion(s32[1024]{0:T(1024)S(1)} %bitcast.97, bf16[1024]{0:T(1024)(128)(2,1)S(1)} %broadcast.132, bf16[]{:T(256)} %constant.11.clone.1), kind=kCustom, calls=%fused_computation.103 | custom fusion | bytes 514 | tf_op jit(solution)/shard_map/scatter | solution.py:85
  31.2 2.3 gather_fusion
  33.5 1.3 bitcast_multiply_fusion
  34.9 25.9 %all_to_all.10 = bf16[32,8,1792]{2,1,0:T(8,128)(2,1)} all-to-all(bf16[32,8,1792]{2,1,0:T(8,128)(2,1)S(1)} %bitcast_multiply_fusion), channel_id=1, replica_groups=mesh['ctx'=32,'ep'=4] {'ctx'}, dimensions={0} | all-to-all | bytes 1835008 | tf_op jit(solution)/shard_map/all_to_all | solution.py:88
  62.2 0.9 slice_reduce_fusion.7
  63.2 87.9 %all_gather.10 = bf16[4096,64]{0,1:T(8,128)(2,1)S(1)} all-gather(bf16[128,64]{0,1:T(8,128)(2,1)S(1)} %copy-done.5), channel_id=1, replica_groups=mesh['ctx'=32,'ep'=4] {'ctx'}, dimensions={0}, use_global_device_ids=true | all-gather | bytes 540672 | tf_op jit(solution)/shard_map/all_gather | solution.py:24
  151.1 1.8 broadcast_compare_fusion
  153.0 5.0 %fusion.12 = f32[256,256]{1,0:T(8,128)} fusion(bf16[256,7168]{1,0:T(8,128)(2,1)} %all-gather.5.cloned.1.call-done, bf16[1,7168,256]{2,1,0:T(8,128)(2,1)} %param.23), kind=kOutput, calls=%fused_computation.28 | convolution fusion | flops 939524096 | bytes 7602176 | tf_op jit(solution)/shard_map/dot_general | solution.py:94
  158.0 10.5 %convolution_convert_fusion.2 = bf16[32,8,7168]{2,1,0:T(8,128)(2,1)} fusion(bf16[1,256,7168]{2,1,0:T(8,128)(2,1)} %param.25, bf16[256,7168]{1,0:T(8,128)(2,1)} %all-gather.5.cloned.1.call-done, bf16[1,7168,256]{2,1,0:T(8,128)(2,1)} %param.24, f32[256,256]{1,0:T(8,128)} %fusion.12), kind=kOutput, calls=%fused_computation.23 | convolution fusion | flops 1881276416 | bytes 14942208 | tf_op jit(solution)/shard_map/dot_general | solution.py:97
  168.5 13.3 %all-to-all-start.1 = ((bf16[32,8,7168]{2,1,0:T(8,128)(2,1)}), bf16[32,8,7168]{2,1,0:T(8,128)(2,1)}, u32[]{:S(2)}, u32[]{:S(2)}) async-start(bf16[32,8,7168]{2,1,0:T(8,128)(2,1)} %convolution_convert_fusion.2), calls=%async_computation.1 | async-start | bytes 7340032 | tf_op jit(solution)/shard_map/all_to_all | solution.py:100
  182.0 30.8 %all-gather.3.cloned.1.call-done = bf16[4096,512]{1,0:T(8,128)(2,1)} async-done(((bf16[128,512]{1,0:T(8,128)(2,1)}), bf16[4096,512]{1,0:T(8,128)(2,1)}) %all-gather.3.cloned.1.call-update) | async-done | bytes 4194320 | tf_op jit(solution)/shard_map/all_gather | solution.py:23
  212.8 14.6 %convolution_convert_fusion.1 = bf16[4096,2048]{0,1:T(8,128)(2,1)} fusion(bf16[4096,512]{1,0:T(8,128)(2,1)} %all-gather.3.cloned.1.call-done, bf16[512,2048]{1,0:T(8,128)(2,1)S(1)} %copy-done), kind=kOutput, calls=%fused_computation.22 | convolution fusion | flops 8598323200 | bytes 23068672 | tf_op jit(solution)/shard_map/dot_general | solution.py:27
  227.4 17.1 %fusion.34 = f32[16,4096,128]{2,1,0:T(8,128)} fusion(bf16[4096,16,128]{0,2,1:T(8,128)(2,1)} %bitcast.88, bf16[128,2048]{1,0:T(8,128)(2,1)S(1)} %copy-done.3), kind=kOutput, calls=%fused_computation.39 | convolution fusion | flops 2147483648 | bytes 50855936 | tf_op jit(solution)/shard_map/qhd,khd->hqk/dot_general | solution.py:36
  244.5 21.6 %fusion.64 = (f32[16,128]{1,0:T(8,128)S(1)}, f32[16,128,4096]{1,2,0:T(8,128)}) fusion(bf16[128,16,64]{0,2,1:T(8,128)(2,1)S(1)} %bitcast.90, bf16[4096,64]{0,1:T(8,128)(2,1)S(1)} %all_gather.10, f32[16,4096,128]{2,1,0:T(8,128)} %fusion.34, pred[128,4096]{0,1:T(8,128)(4,1)S(1)} %broadcast_compare_fusion), kind=kOutput, calls=%fused_computation.107 | convolution fusion | flops 1107294208 | bytes 68427776 | tf_op jit(solution)/shard_map/qhd,kd->hqk/dot_general | solution.py:39
  266.1 13.8 %fusion.2 = f32[16,128]{1,0:T(8,128)S(1)} fusion(f32[16,128,4096]{1,2,0:T(8,128)} %get-tuple-element.29, f32[16,128]{1,0:T(8,128)S(1)} %broadcast_maximum_fusion, pred[128,4096]{0,1:T(8,128)(4,1)S(1)} %broadcast_compare_fusion), kind=kLoop, calls=%fused_computation.15 | loop fusion | flops 25163776 | bytes 34095104 | tf_op jit(solution)/shard_map/reduce_sum | solution.py:46
  279.9 5.9 %bitcast_convert_fusion = f32[256,7168]{1,0:T(8,128)} fusion(bf16[32,8,7168]{2,1,0:T(8,128)(2,1)} %all-to-all-done.1), kind=kLoop, calls=%fused_computation.24 | loop fusion | flops 1835008 | bytes 11010048 | tf_op jit(solution)/shard_map/reshape | solution.py:108
  285.8 8.1 %gather_fusion.1 = f32[128,7168]{1,0:T(8,128)} fusion(f32[256,7168]{1,0:T(8,128)} %bitcast_convert_fusion, s32[1024]{0:T(1024)S(1)} %get-tuple-element.37), kind=kCustom, calls=%fused_computation.1 | custom fusion | bytes 7340544 | tf_op jit(solution)/shard_map/gather | solution.py:64
  293.9 8.1 %gather_fusion.2 = f32[128,7168]{1,0:T(8,128)} fusion(f32[256,7168]{1,0:T(8,128)} %bitcast_convert_fusion, s32[1024]{0:T(1024)S(1)} %get-tuple-element.36), kind=kCustom, calls=%fused_computation.2 | custom fusion | bytes 7340544 | tf_op jit(solution)/shard_map/gather | solution.py:64
  301.9 8.1 %gather_fusion.3 = f32[128,7168]{1,0:T(8,128)} fusion(f32[256,7168]{1,0:T(8,128)} %bitcast_convert_fusion, s32[1024]{0:T(1024)S(1)} %get-tuple-element.35), kind=kCustom, calls=%fused_computation.3 | custom fusion | bytes 7340544 | tf_op jit(solution)/shard_map/gather | solution.py:64
  310.0 8.1 %gather_fusion.4 = f32[128,7168]{1,0:T(8,128)} fusion(f32[256,7168]{1,0:T(8,128)} %bitcast_convert_fusion, s32[1024]{0:T(1024)S(1)} %get-tuple-element.34), kind=kCustom, calls=%fused_computation.4 | custom fusion | bytes 7340544 | tf_op jit(solution)/shard_map/gather | solution.py:64
  318.1 8.5 %gather_fusion.5 = f32[128,7168]{1,0:T(8,128)} fusion(f32[256,7168]{1,0:T(8,128)} %bitcast_convert_fusion, s32[1024]{0:T(1024)S(1)} %get-tuple-element.33), kind=kCustom, calls=%fused_computation.5 | custom fusion | bytes 7340544 | tf_op jit(solution)/shard_map/gather | solution.py:64
  326.6 8.1 %gather_fusion.6 = f32[128,7168]{1,0:T(8,128)} fusion(f32[256,7168]{1,0:T(8,128)} %bitcast_convert_fusion, s32[1024]{0:T(1024)S(1)} %get-tuple-element.32), kind=kCustom, calls=%fused_computation.6 | custom fusion | bytes 7340544 | tf_op jit(solution)/shard_map/gather | solution.py:64
  334.7 8.1 %gather_fusion.7 = f32[128,7168]{1,0:T(8,128)} fusion(f32[256,7168]{1,0:T(8,128)} %bitcast_convert_fusion, s32[1024]{0:T(1024)S(1)} %get-tuple-element.31), kind=kCustom, calls=%fused_computation.7 | custom fusion | bytes 7340544 | tf_op jit(solution)/shard_map/gather | solution.py:64
  342.9 8.1 %gather_fusion.8 = f32[128,7168]{1,0:T(8,128)} fusion(f32[256,7168]{1,0:T(8,128)} %bitcast_convert_fusion, s32[1024]{0:T(1024)S(1)} %get-tuple-element.30), kind=kCustom, calls=%fused_computation.8 | custom fusion | bytes 7340544 | tf_op jit(solution)/shard_map/gather | solution.py:64
  351.0 12.7 %add_convert_fusion = bf16[128,7168]{1,0:T(8,128)(2,1)} fusion(f32[128,7168]{1,0:T(8,128)} %gather_fusion.8, f32[128,7168]{1,0:T(8,128)} %gather_fusion.7, f32[128,7168]{1,0:T(8,128)} %gather_fusion.6, f32[128,7168]{1,0:T(8,128)} %gather_fusion.5, f32[128,7168]{1,0:T(8,128)} %gather_fusion.4, f32[128,7168]{1,0:T(8,128)} %gather_fusion.3, ...), kind=kLoop, calls=%fused_computation.30 | loop fusion | flops 14680064 | bytes 31199232 | tf_op jit(solution)/shard_map/convert_element_type | solution.py:111
  363.8 14.6 %convolution_convert_fusion = bf16[4096,2048]{0,1:T(8,128)(2,1)} fusion(bf16[4096,512]{1,0:T(8,128)(2,1)} %all-gather.3.cloned.1.call-done, bf16[512,2048]{1,0:T(8,128)(2,1)S(1)} %copy-done.15), kind=kOutput, calls=%fused_computation.21 | convolution fusion | flops 8598323200 | bytes 23068672 | tf_op jit(solution)/shard_map/dot_general | solution.py:32
  378.4 18.5 %fusion.31 = bf16[128,16,128]{0,2,1:T(8,128)(2,1)S(1)} fusion(bf16[4096,16,128]{0,2,1:T(8,128)(2,1)} %bitcast.98, f32[16,128,4096]{1,2,0:T(8,128)} %get-tuple-element.29, f32[16,128]{1,0:T(8,128)S(1)} %broadcast_maximum_fusion, pred[128,4096]{0,1:T(8,128)(4,1)S(1)} %broadcast_compare_fusion, f32[128,16]{0,1:T(8,128)S(1)} %bitcast.95), kind=kOutput, calls=%fused_computation.36 | convolution fusion | flops 2173173760 | bytes 51396608 | tf_op jit(solution)/shard_map/hqk,khd->hqd/dot_general | solution.py:47
  396.9 1.0 copy.43
  (73 shorter events, 3.0 us)
Async XLA Ops:
  7.2 205.6 %copy-start = (bf16[512,2048]{1,0:T(8,128)(2,1)S(1)}, bf16[512,2048]{1,0:T(8,128)(2,1)}, u32[]{:S(2)}) copy-start(bf16[512,2048]{1,0:T(8,128)(2,1)} %param.17) | copy-start | bytes 6291460
  7.2 24.1 %copy-start.2 = (bf16[128,1792]{1,0:T(8,128)(2,1)S(1)}, bf16[128,1792]{1,0:T(8,128)(2,1)}, u32[]{:S(2)}) copy-start(bf16[128,1792]{1,0:T(8,128)(2,1)} %param.20) | copy-start | bytes 1376260
  7.2 145.8 %all-gather.5.cloned.1.call-start = ((), (), s32[]{:S(2)}) async-start(), calls=%async_computation.4 | async-start | bytes 4587520 | tf_op jit(solution)/shard_map/all_gather | solution.py:93
  33.5 28.0 %copy-start.4 = (bf16[128,1024]{1,0:T(8,128)(2,1)S(1)}, bf16[128,1024]{1,0:T(8,128)(2,1)}, u32[]{:S(2)}) copy-start(bf16[128,1024]{1,0:T(8,128)(2,1)} %param.14) | copy-start | bytes 786436
  33.5 28.2 %copy-start.6 = (s32[4096]{0:T(1024)S(1)}, s32[4096]{0:T(1024)}, u32[]{:S(2)}) copy-start(s32[4096]{0:T(1024)} %param.19) | copy-start | bytes 49156
  33.5 29.7 %copy-start.5 = (bf16[128,64]{0,1:T(8,128)(2,1)S(1)}, bf16[128,64]{0,1:T(8,128)(2,1)}, u32[]{:S(2)}) copy-start(bf16[128,64]{0,1:T(8,128)(2,1)} %param.16) | copy-start | bytes 49156
  60.8 152.0 %all-gather.3.cloned.1.call-start = ((), (), s32[]{:S(2)}) async-start(), calls=%async_computation.3 | async-start | bytes 4325376 | tf_op jit(solution)/shard_map/all_gather | solution.py:23
  168.5 111.4 %all-to-all-start.1 = ((bf16[32,8,7168]{2,1,0:T(8,128)(2,1)}), bf16[32,8,7168]{2,1,0:T(8,128)(2,1)}, u32[]{:S(2)}, u32[]{:S(2)}) async-start(bf16[32,8,7168]{2,1,0:T(8,128)(2,1)} %convolution_convert_fusion.2), calls=%async_computation.1 | async-start | bytes 7340032 | tf_op jit(solution)/shard_map/all_to_all | solution.py:100
  181.8 216.1 %reduce-scatter.2.cloned.1.call-start = ((), (), s32[]{:S(2)}) async-start(), calls=%async_computation.5 | async-start | bytes 2293760 | tf_op jit(solution)/shard_map/reduce_scatter | solution.py:110
  212.8 14.6 %copy-start.3 = (bf16[128,2048]{1,0:T(8,128)(2,1)S(1)}, bf16[128,2048]{1,0:T(8,128)(2,1)}, u32[]{:S(2)}) copy-start(bf16[128,2048]{1,0:T(8,128)(2,1)} %param.13) | copy-start | bytes 1572868
  342.8 8.1 %copy-start.7 = (f32[128]{0:T(128)S(1)}, f32[128]{0:T(128)}, u32[]{:S(2)}) copy-start(f32[128]{0:T(128)} %get-tuple-element.8) | copy-start | bytes 1540
  342.8 8.1 %copy-start.8 = (f32[128]{0:T(128)S(1)}, f32[128]{0:T(128)}, u32[]{:S(2)}) copy-start(f32[128]{0:T(128)} %get-tuple-element.9) | copy-start | bytes 1540
  342.8 8.1 %copy-start.9 = (f32[128]{0:T(128)S(1)}, f32[128]{0:T(128)}, u32[]{:S(2)}) copy-start(f32[128]{0:T(128)} %get-tuple-element.10) | copy-start | bytes 1540
  342.8 8.1 %copy-start.10 = (f32[128]{0:T(128)S(1)}, f32[128]{0:T(128)}, u32[]{:S(2)}) copy-start(f32[128]{0:T(128)} %get-tuple-element.11) | copy-start | bytes 1540
  342.8 8.1 %copy-start.11 = (f32[128]{0:T(128)S(1)}, f32[128]{0:T(128)}, u32[]{:S(2)}) copy-start(f32[128]{0:T(128)} %get-tuple-element.12) | copy-start | bytes 1540
  342.8 8.1 %copy-start.12 = (f32[128]{0:T(128)S(1)}, f32[128]{0:T(128)}, u32[]{:S(2)}) copy-start(f32[128]{0:T(128)} %get-tuple-element.13) | copy-start | bytes 1540
  342.9 8.1 %copy-start.13 = (f32[128]{0:T(128)S(1)}, f32[128]{0:T(128)}, u32[]{:S(2)}) copy-start(f32[128]{0:T(128)} %get-tuple-element.14) | copy-start | bytes 1540
  342.9 8.1 %copy-start.14 = (f32[128]{0:T(128)S(1)}, f32[128]{0:T(128)}, u32[]{:S(2)}) copy-start(f32[128]{0:T(128)} %get-tuple-element.15) | copy-start | bytes 1540
  351.0 12.8 %copy-start.15 = (bf16[512,2048]{1,0:T(8,128)(2,1)S(1)}, bf16[512,2048]{1,0:T(8,128)(2,1)}, u32[]{:S(2)}) copy-start(bf16[512,2048]{1,0:T(8,128)(2,1)} %param.18) | copy-start | bytes 6291460
  378.4 19.5 %copy-start.1 = (bf16[512,2048]{1,0:T(8,128)(2,1)S(1)}, bf16[512,2048]{1,0:T(8,128)(2,1)}, u32[]{:S(2)}) copy-start(bf16[512,2048]{1,0:T(8,128)(2,1)} %param.17) | copy-start | bytes 6291460
Sparse Core Ops, SparseCore 0:
  60.9 39.5 all-gather.4
  103.5 109.2 all-gather.2
  363.9 23.1 reduce-scatter.1
where the time goes:
time: 411 us; the launch traced here: 405 us
  blocking collectives  114 us (28%)
  matrix products  102 us (25%)
  local copies, waits for them, and re-layouts  84.2 us (20%)
  other arithmetic  45.3 us (11%)
  waiting for transfers between devices  31.6 us (8%)
  between operations  14.3 us (3%)
  starting transfers between devices  13.6 us (3%)
    all_gather x1, blocking collectives, latent_attention(): block_rope = lax.all_gather(k_rope, 'ctx', axis=0, tiled=True)  87.9 us
    gather x8, local copies, waits for them, and re-layouts, weighted_sum(): slot_values[gather_index[:, choice_slot]]  65.1 us
    all_gather x1, waiting for transfers between devices, latent_attention(): block_latent = lax.all_gather(latent, 'ctx', axis=0, tiled=True)  30.8 us
    all_to_all x1, blocking collectives, expert_layer(): lax.all_to_all(outgoing, 'ctx', split_axis=0, concat_axis=0, tiled=True)  25.9 us
    dot_general x1, matrix products, latent_attention(): jnp.einsum('qhd,kd->hqk', query_rope, block_rope, preferred_element_type=...  21.6 us
    dot_general x1, matrix products, latent_attention(): jnp.einsum('hqk,khd->hqd', weights_exp.astype(jnp.bfloat16), block_values...  18.5 us
    dot_general x1, matrix products, latent_attention(): jnp.einsum('qhd,khd->hqk', query_nope, keys_nope, preferred_element_type=...  17.1 us
    dot_general x1, matrix products, latent_attention(): jnp.dot(block_latent, w_uk, preferred_element_type=jnp.float32)  14.6 us
  transfers between devices with their start and end apart: 4, of which 1 were waited for; matrix products, arithmetic and copies ran while one was open for 30% of the time, Pallas kernels for 0%

commit v1 on v0

v1 whole, which is shorter than its diff:
```python
import math

import jax
import jax.numpy as jnp
from jax import lax
from jax.experimental import pallas as pl
from jax.experimental.pallas import tpu as pltpu
from jax.sharding import PartitionSpec as P

F32 = jnp.float32
BF16 = jnp.bfloat16
MESH = pl.DeviceIdType.MESH

NOPE = 128
ROPE = 64
LAT = 512
CAP = 8
N_CTX = 32
KW = LAT + 2 * ROPE
RUN = 64
GROUP = 256
SCALE = 1.0 / math.sqrt(NOPE + ROPE)
LOG2E = math.log2(math.e)
LOW = -1e30


def dot(a, b):
    return jnp.dot(a, b, preferred_element_type=F32)


def dot_t(a, b):
    return lax.dot_general(a, b, (((1,), (1,)), ((), ())), preferred_element_type=F32)


def iota(shape, dim):
    return lax.broadcasted_iota(jnp.int32, shape, dim)


def kernel(
    meta,
    latent,
    k_rope,
    rows,
    ids,
    weights,
    q_nope_h,
    q_rope_h,
    w_uk_h,
    w_uv_h,
    w_gate_h,
    w_up_h,
    w_down_h,
    attn_out,
    moe_out,
    q_nope,
    q_rope,
    w_uk,
    w_uv,
    w_gate,
    w_up,
    w_down,
    outgoing,
    slots,
    to_mate,
    from_mate,
    to_pair,
    kept,
    from_pair,
    going,
    returned,
    keys,
    key_group,
    queries,
    acc,
    row_max,
    row_sum,
    load_sem,
    disp_send,
    disp_recv,
    pair_send,
    pair_recv,
    core_send,
    core_recv,
    ag_send,
    ag_recv,
    back_core_send,
    back_core_recv,
    back_pair_send,
    back_pair_recv,
    back_send,
    back_recv,
):
    ctx = lax.axis_index("ctx")
    ep = lax.axis_index("ep")
    h = ctx // 16
    z = (ctx // 4) % 4
    y = ctx % 4
    lo = ep // 2
    core = ep % 2
    ep_pair = (1 - lo) * 2 + core
    ep_mate = lo * 2 + (1 - core)
    part = rows.shape[1]
    half = part // 2

    def context(step, dz, dy):
        other = h if step == 0 else 1 - h
        return other * 16 + ((z + dz) % 4) * 4 + (y + dy) % 4

    def partner_ep(step):
        return ep if step == 0 else ep_pair

    def window(step):
        return (h if step == 0 else 1 - h) * 16

    def kept_lo(step):
        return lo if step == 0 else 1 - lo

    order = [(s, dz, dy) for s in range(2) for dz in (0, 1, 3, 2) for dy in (0, 1, 3, 2)]

    loads = [
        pltpu.make_async_copy(src, dst, load_sem.at[i])
        for i, (src, dst) in enumerate(
            (
                (q_nope_h, q_nope),
                (q_rope_h, q_rope),
                (w_uk_h, w_uk),
                (w_gate_h.at[0], w_gate),
                (w_up_h.at[0], w_up),
                (w_down_h.at[0], w_down),
                (w_uv_h, w_uv),
            )
        )
    ]
    for load in loads:
        load.start()

    barrier = pltpu.get_barrier_semaphore()
    for s, dz, dy in order[1:]:
        pl.semaphore_signal(
            barrier, inc=1, device_id=(context(s, dz, dy), partner_ep(s)), device_id_type=MESH
        )
    pl.semaphore_signal(barrier, inc=1, device_id=(ctx, ep_pair), device_id_type=MESH)
    pl.semaphore_signal(barrier, inc=1, device_id=(ctx, ep_mate), device_id_type=MESH)

    lane = iota((128, 128), 1)
    named = jnp.zeros((128, 128), F32)
    slot_weight = jnp.zeros((128, 128), F32)
    for k in range(ids.shape[1]):
        hit = (ids[:, k : k + 1] == lane) & (lane < N_CTX)
        named = jnp.where(hit, 1.0, named)
        slot_weight = jnp.where(hit, weights[:, k : k + 1], slot_weight)
    earlier = jnp.where(lane < iota((128, 128), 0), 1.0, 0.0).astype(BF16)
    rank = dot(earlier, named.astype(BF16))
    named_b = named.astype(BF16)
    rank_b = rank.astype(BF16)
    spread = jnp.where(iota((256, 128), 0) // CAP == iota((256, 128), 1), 1.0, 0.0).astype(BF16)
    picked = (dot_t(spread, named_b) > 0.5) & (
        dot_t(spread, rank_b) == (iota((256, 128), 0) % CAP).astype(F32)
    )
    pick = jnp.where(picked, 1.0, 0.0).astype(BF16)
    for c in range(4):
        lhs = pick[64 * c : 64 * (c + 1)]
        first = dot(lhs, rows[:, :half]).reshape(8, CAP, half)
        second = dot(lhs, rows[:, half:]).reshape(8, CAP, half)
        outgoing[8 * c : 8 * (c + 1)] = jnp.concatenate([first, second], axis=1).astype(BF16)

    double = jnp.where(iota((64, 128), 1) % ROPE == iota((64, 128), 0), 1.0, 0.0).astype(BF16)
    own_rows = pl.ds(pl.multiple_of(core * RUN, RUN), RUN)
    major = jnp.where(core == 0, z, y)
    minor = jnp.where(core == 0, y, z)
    keys[core, h, major * 4 + minor, :, :LAT] = latent[own_rows, :]
    keys[core, h, major * 4 + minor, :, LAT:] = dot(k_rope[own_rows, :], double).astype(BF16)

    pl.semaphore_wait(barrier, 33)

    own = pltpu.make_async_copy(outgoing.at[ctx], slots.at[ep, ctx], disp_recv.at[0, 0])
    own.start()
    for s, dz, dy in order[1:]:
        to = context(s, dz, dy)
        pltpu.make_async_remote_copy(
            src_ref=outgoing.at[to],
            dst_ref=slots.at[ep, ctx],
            send_sem=disp_send.at[0],
            recv_sem=disp_recv.at[s, dz],
            device_id=(to, partner_ep(s)),
            device_id_type=MESH,
        ).start()

    def at_axis(major_to, minor_to):
        z_to = jnp.where(core == 0, major_to, minor_to)
        y_to = jnp.where(core == 0, minor_to, major_to)
        return h * 16 + z_to * 4 + y_to

    pltpu.make_async_remote_copy(
        src_ref=keys.at[core, h, major * 4 + minor],
        dst_ref=keys.at[core, h, major * 4 + minor],
        send_sem=ag_send.at[0],
        recv_sem=ag_recv.at[0],
        device_id=((1 - h) * 16 + z * 4 + y, ep_pair),
        device_id_type=MESH,
    ).start()

    def wait_for(ref, sem):
        pltpu.make_async_copy(ref, ref, sem).wait()

    for load in loads[:3]:
        load.wait()
    even = iota((1, 128), 1) < ROPE

    @pl.loop(0, 8)
    def _(pair):
        at = pl.ds(pl.multiple_of(pair * 128, 128), 128)
        rope = q_rope[:, at].astype(F32)
        for which in range(2):
            cols = pl.ds(pl.multiple_of(pair * 256 + which * 128, 128), 128)
            lat = dot_t(q_nope[:, cols], w_uk[:, cols]).astype(BF16)
            rot = jnp.where(even if which == 0 else ~even, rope, 0.0).astype(BF16)
            to = pl.ds(pl.multiple_of(pair * 128 + which * 64, 64), 64)
            for run in range(2):
                queries[run, to, :LAT] = lat[run * 64 : (run + 1) * 64]
                queries[run, to, LAT:] = rot[run * 64 : (run + 1) * 64]

    def chunk(step, dz, lo_part):
        return slots.at[lo_part * 2 + core, pl.ds(window(step) + ((z - dz + 4) % 4) * 4, 4)]

    def relay(step, dz):
        region = chunk(step, dz, kept_lo(step))
        wait_for(region, disp_recv.at[step, dz])
        pltpu.make_async_remote_copy(
            src_ref=region,
            dst_ref=region,
            send_sem=pair_send.at[0],
            recv_sem=pair_recv.at[step, dz],
            device_id=(ctx, ep_pair),
            device_id_type=MESH,
        ).start()
        pltpu.make_async_remote_copy(
            src_ref=region,
            dst_ref=region,
            send_sem=core_send.at[0],
            recv_sem=core_recv.at[0, step],
            device_id=(ctx, ep_mate),
            device_id_type=MESH,
        ).start()

    def relay_again(step, dz):
        region = chunk(step, dz, 1 - kept_lo(step))
        wait_for(region, pair_recv.at[step, dz])
        pltpu.make_async_remote_copy(
            src_ref=region,
            dst_ref=region,
            send_sem=core_send.at[0],
            recv_sem=core_recv.at[1, step],
            device_id=(ctx, ep_mate),
            device_id_type=MESH,
        ).start()

    def keys_second():
        wait_for(keys.at[core, 1 - h, major * 4 + minor], ag_recv.at[0])
        for t in (1, 3, 2):
            region = keys.at[core, :, major * 4 + minor]
            pltpu.make_async_remote_copy(
                src_ref=region,
                dst_ref=region,
                send_sem=ag_send.at[1],
                recv_sem=ag_recv.at[1],
                device_id=(at_axis(major, (minor + t) % 4), ep),
                device_id_type=MESH,
            ).start()

    def keys_to_mate(at):
        region = keys.at[core, :, pl.ds(at * 4, 4)]
        pltpu.make_async_remote_copy(
            src_ref=region,
            dst_ref=region,
            send_sem=ag_send.at[3],
            recv_sem=ag_recv.at[5],
            device_id=(ctx, ep_mate),
            device_id_type=MESH,
        ).start()

    def keys_third():
        wait_for(keys.at[core, :, pl.ds(0, 3)], ag_recv.at[1])
        region = keys.at[core, :, pl.ds(major * 4, 4)]
        for t in (1, 3, 2):
            pltpu.make_async_remote_copy(
                src_ref=region,
                dst_ref=region,
                send_sem=ag_send.at[2],
                recv_sem=ag_recv.at[1 + t],
                device_id=(at_axis((major + t) % 4, minor), ep),
                device_id_type=MESH,
            ).start()
        keys_to_mate(major)

    def keys_share(t):
        at = (major - t + 4) % 4
        wait_for(keys.at[core, :, pl.ds(at * 4, 4)], ag_recv.at[1 + t])
        keys_to_mate(at)

    relay(0, 0)
    keys_second()
    relay(0, 1)
    relay(0, 3)
    relay(0, 2)
    keys_third()
    for dz in (0, 1, 3, 2):
        relay(1, dz)
    for dz in (0, 1, 3, 2):
        relay_again(0, dz)
    for load in loads[3:]:
        load.wait()

    def from_experts(step):
        start = window(step)
        for j in range(2):
            lo_part = kept_lo(step) if j == 0 else 1 - kept_lo(step)
            wait_for(
                slots.at[lo_part * 2 + (1 - core), pl.ds(start, 16)], core_recv.at[j, step]
            )

        def some(p, carry):
            gate, up = carry
            taken = slots[p, pl.ds(start, 16)].astype(F32)
            for i in range(2):
                x = taken[:, CAP * i : CAP * (i + 1)].reshape(128, half).astype(BF16)
                at = pl.ds(pl.multiple_of(p * part + i * half, 128), half)
                gate = gate + dot(x, w_gate[at, :])
                up = up + dot(x, w_up[at, :])
            return gate, up

        width = w_gate.shape[1]
        gate, up = lax.fori_loop(
            0, 4, some, (jnp.zeros((128, width), F32), jnp.zeros((128, width), F32))
        )
        hidden = (gate / (1.0 + jnp.exp(-gate)) * up).astype(BF16)

        def through_down(p):
            both = []
            for i in range(2):
                at = pl.ds(pl.multiple_of(p * part + i * half, 128), half)
                both.append(dot(hidden, w_down[:, at]).reshape(16, CAP, half))
            return jnp.concatenate(both, axis=1)

        for j in range(2):
            lo_part = 1 - kept_lo(step) if j == 0 else kept_lo(step)
            to_mate[step, j] = through_down(lo_part * 2 + (1 - core)).astype(BF16)
            pltpu.make_async_remote_copy(
                src_ref=to_mate.at[step, j],
                dst_ref=from_mate.at[step, j],
                send_sem=back_core_send.at[step, j],
                recv_sem=back_core_recv.at[step, j],
                device_id=(ctx, ep_mate),
                device_id_type=MESH,
            ).start()
        mine = through_down((1 - kept_lo(step)) * 2 + core)
        wait_for(from_mate.at[step, 0], back_core_recv.at[step, 0])
        to_pair[step] = (mine + from_mate[step, 0].astype(F32)).astype(BF16)
        pltpu.make_async_remote_copy(
            src_ref=to_pair.at[step],
            dst_ref=from_pair.at[step],
            send_sem=back_pair_send.at[step],
            recv_sem=back_pair_recv.at[step],
            device_id=(ctx, ep_pair),
            device_id_type=MESH,
        ).start()
        mine = through_down(kept_lo(step) * 2 + core)
        wait_for(from_mate.at[step, 1], back_core_recv.at[step, 1])
        kept[step] = (mine + from_mate[step, 1].astype(F32)).astype(BF16)

    def send_back(step):
        wait_for(from_pair.at[step], back_pair_recv.at[step])
        going[step] = (kept[step].astype(F32) + from_pair[step].astype(F32)).astype(BF16)
        for s, dz, dy in order:
            if s != step:
                continue
            to = context(s, dz, dy)
            at = ((z + dz) % 4) * 4 + (y + dy) % 4
            if (s, dz, dy) == (0, 0, 0):
                pltpu.make_async_copy(going.at[0, at], returned.at[ctx], back_recv.at[0]).start()
                continue
            pltpu.make_async_remote_copy(
                src_ref=going.at[s, at],
                dst_ref=returned.at[ctx],
                send_sem=back_send.at[0],
                recv_sem=back_recv.at[s],
                device_id=(to, partner_ep(s)),
                device_id_type=MESH,
            ).start()

    run_0 = meta[64 + 2 * ctx]
    run_1 = meta[64 + 2 * ctx + 1]
    run_late = jnp.maximum(run_0, run_1)
    run_early = jnp.minimum(run_0, run_1)
    late_half = jnp.where(run_1 > run_0, 1, 0)
    late_steps = run_late // 4 + 1
    heads_rows = queries.shape[1]
    blocks = heads_rows // 256

    row_max[...] = jnp.full(row_max.shape, LOW, F32)
    row_sum[...] = jnp.zeros(row_sum.shape, F32)
    acc[...] = jnp.zeros(acc.shape, F32)

    def attend(i, kind):
        is_late = i < late_steps
        if kind == "late":
            side, group, q_half, q_run = 1, i, late_half, run_late
        elif kind == "early":
            side, group, q_half, q_run = 0, i - late_steps, 1 - late_half, run_early
        else:
            side = jnp.where(is_late, 1, 0)
            group = jnp.where(is_late, i, i - late_steps)
            q_half = jnp.where(is_late, late_half, 1 - late_half)
            q_run = jnp.where(is_late, run_late, run_early)
        for t in range(4):
            at = meta[group * 4 + t]
            key_group[t * RUN : (t + 1) * RUN, :] = keys[at // 32, (at // 16) % 2, at % 16]
        key_pos = group * GROUP + iota((256, 256), 1)
        query_pos = q_run * RUN + iota((256, 256), 0) % RUN
        for b in range(blocks):
            at = slice(b * 256, (b + 1) * 256)
            scores = dot_t(queries[q_half, at, :], key_group[...])
            if masked(kind):
                scores = jnp.where(key_pos <= query_pos, scores, LOW)
            old_max = row_max[side, at, :]
            new_max = jnp.maximum(old_max, jnp.max(scores, axis=1, keepdims=True))
            fade = jnp.exp2((old_max - new_max) * (SCALE * LOG2E))
            probs = jnp.exp2(
                (scores - jnp.concatenate([new_max, new_max], axis=1)) * (SCALE * LOG2E)
            )
            new_sum = row_sum[side, at, :] * fade + (probs[:, :128] + probs[:, 128:])
            new_acc = acc[side, at, :] * jnp.concatenate([fade] * 4, axis=1) + dot(
                probs.astype(BF16), key_group[:, :LAT]
            )
            if kind == "any":
                for to in range(2):
                    here = side == to
                    row_max[to, at, :] = jnp.where(here, new_max, row_max[to, at, :])
                    row_sum[to, at, :] = jnp.where(here, new_sum, row_sum[to, at, :])
                    acc[to, at, :] = jnp.where(here, new_acc, acc[to, at, :])
            else:
                row_max[side, at, :] = new_max
                row_sum[side, at, :] = new_sum
                acc[side, at, :] = new_acc

    def masked(kind):
        return kind != "late"

    from_experts(0)
    for dz in (0, 1, 3, 2):
        relay_again(1, dz)
    from_experts(1)
    keys_share(1)
    keys_share(3)
    keys_share(2)
    wait_for(keys.at[1 - core], ag_recv.at[5])

    @pl.loop(0, 4)
    def _(i):
        attend(i, "late")

    send_back(0)

    @pl.loop(4, 8)
    def _(i):
        attend(i, "late")

    @pl.loop(8, 12)
    def _(i):
        attend(i, "any")

    send_back(1)

    @pl.loop(12, 16)
    def _(i):
        attend(i, "any")

    attend(jnp.int32(16), "early")

    first_side = jnp.where(run_0 > run_1, 1, 0)

    @pl.loop(0, 16)
    def _(head):
        at = pl.ds(pl.multiple_of(head * 64, 64), 64)
        cols = pl.ds(pl.multiple_of(head * 128, 128), 128)
        both = []
        for side in (first_side, 1 - first_side):
            total = jnp.sum(row_sum[side, at, :], axis=1, keepdims=True)
            both.append(acc[side, at, :] / total)
        mixed = jnp.concatenate(both, axis=0).astype(BF16)
        attn_out[:, cols] = dot(mixed, w_uv[:, cols]).astype(BF16)

    wide = (128, N_CTX * 2 * CAP)
    column = iota(wide, 1)
    spread_2 = jnp.where(column // (2 * CAP) == iota(wide, 0), 1.0, 0.0).astype(BF16)
    weight_hi = slot_weight.astype(BF16)
    weight_lo = (slot_weight - weight_hi.astype(F32)).astype(BF16)
    here = (dot(named_b, spread_2) > 0.5) & (
        dot(rank_b, spread_2) == (column % CAP).astype(F32)
    )
    parts = [dot(w, spread_2) for w in (weight_hi, weight_lo)]
    wait_for(returned.at[pl.ds(0, 16)], back_recv.at[0])
    wait_for(returned.at[pl.ds(0, 16)], back_recv.at[1])
    for i in range(2):
        mine = here & ((column // CAP) % 2 == i)
        total = jnp.zeros((128, half), F32)
        for w in parts:
            factor = jnp.where(mine, w, 0.0).astype(BF16)
            total = total + dot(factor, returned[...].reshape(N_CTX * 2 * CAP, half))
        moe_out[:, i * half : (i + 1) * half] = total.astype(BF16)

    wait_for(outgoing.at[pl.ds(0, 31)], disp_send.at[0])
    wait_for(slots.at[0], pair_send.at[0])
    wait_for(slots.at[pl.ds(0, 2)], core_send.at[0])
    wait_for(keys.at[0, 0, 0], ag_send.at[0])
    wait_for(keys.at[0, :, pl.ds(0, 3)], ag_send.at[1])
    wait_for(keys.at[0, :, pl.ds(0, 12)], ag_send.at[2])
    wait_for(keys.at[0], ag_send.at[3])
    for step in range(2):
        for j in range(2):
            wait_for(to_mate.at[step, j], back_core_send.at[step, j])
        wait_for(to_pair.at[step], back_pair_send.at[step])
    wait_for(outgoing.at[pl.ds(0, 31)], back_send.at[0])


def shards(
    q_nope,
    q_rope,
    latent,
    k_rope,
    w_uk,
    w_uv,
    positions,
    moe_rows,
    expert_ids,
    expert_weights,
    w_gate,
    w_up,
    w_down,
):
    runs = positions[::RUN] // RUN
    pairs = runs.reshape(N_CTX, 2)
    placed = jnp.concatenate(
        [pairs[:, 0], pairs[:, 1].reshape(2, 4, 4).transpose(0, 2, 1).reshape(N_CTX)]
    )
    spots = jnp.arange(2 * N_CTX, dtype=jnp.int32)
    where = jnp.sum(jnp.where(placed[None, :] == spots[:, None], spots[None, :], 0), axis=1)
    meta = jnp.concatenate([where, runs]).astype(jnp.int32)

    count, part = moe_rows.shape
    half = part // 2
    vmem = pl.BlockSpec(memory_space=pltpu.VMEM)
    anywhere = pl.BlockSpec(memory_space=pl.ANY)
    dma = pltpu.SemaphoreType.DMA
    heads_rows = q_nope.shape[1] // NOPE * RUN
    slot = (2 * CAP, half)
    return pl.pallas_call(
        kernel,
        out_shape=(
            jax.ShapeDtypeStruct(q_nope.shape, BF16),
            jax.ShapeDtypeStruct(moe_rows.shape, BF16),
        ),
        in_specs=[pl.BlockSpec(memory_space=pltpu.SMEM)] + [vmem] * 5 + [anywhere] * 7,
        out_specs=(vmem, vmem),
        scratch_shapes=[
            pltpu.VMEM(q_nope.shape, BF16),
            pltpu.VMEM(q_rope.shape, BF16),
            pltpu.VMEM(w_uk.shape, BF16),
            pltpu.VMEM(w_uv.shape, BF16),
            pltpu.VMEM(w_gate.shape[1:], BF16),
            pltpu.VMEM(w_up.shape[1:], BF16),
            pltpu.VMEM(w_down.shape[1:], BF16),
            pltpu.VMEM((N_CTX,) + slot, BF16),
            pltpu.VMEM((4, N_CTX) + slot, BF16),
            pltpu.VMEM((2, 2, 16) + slot, BF16),
            pltpu.VMEM((2, 2, 16) + slot, BF16),
            pltpu.VMEM((2, 16) + slot, BF16),
            pltpu.VMEM((2, 16) + slot, BF16),
            pltpu.VMEM((2, 16) + slot, BF16),
            pltpu.VMEM((2, 16) + slot, BF16),
            pltpu.VMEM((N_CTX,) + slot, BF16),
            pltpu.VMEM((2, 2, 16, RUN, KW), BF16),
            pltpu.VMEM((GROUP, KW), BF16),
            pltpu.VMEM((2, heads_rows, KW), BF16),
            pltpu.VMEM((2, heads_rows, LAT), F32),
            pltpu.VMEM((2, heads_rows, 128), F32),
            pltpu.VMEM((2, heads_rows, 128), F32),
            dma((7,)),
            dma((1,)),
            dma((2, 4)),
            dma((1,)),
            dma((2, 4)),
            dma((1,)),
            dma((2, 2)),
            dma((4,)),
            dma((6,)),
            dma((2, 2)),
            dma((2, 2)),
            dma((2,)),
            dma((2,)),
            dma((1,)),
            dma((2,)),
        ],
        compiler_params=pltpu.CompilerParams(
            collective_id=0, has_side_effects=True, vmem_limit_bytes=56 * 1024 * 1024
        ),
        name="attend_and_dispatch",
    )(
        meta,
        latent,
        k_rope,
        moe_rows,
        expert_ids,
        expert_weights,
        q_nope,
        q_rope,
        w_uk,
        w_uv,
        w_gate,
        w_up,
        w_down,
    )


def solution(mesh):
    return jax.shard_map(
        shards,
        mesh=mesh,
        in_specs=(
            P("ctx", "ep"),
            P("ctx", "ep"),
            P("ctx", None),
            P("ctx", None),
            P(None, "ep"),
            P(None, "ep"),
            P(),
            P("ctx", "ep"),
            P("ctx", None),
            P("ctx", None),
            P("ctx", None, "ep"),
            P("ctx", None, "ep"),
            P("ctx", "ep", None),
        ),
        out_specs=(P("ctx", "ep"), P("ctx", "ep")),
        check_vma=False,
    )
```

time: 411 us -> 109 us (0.27)
  the two profiles are of different devices: /device:TPU:24 before, /device:TPU:1 now
where the time goes in v1:
time: 109 us
  Pallas kernels  97.8 us (90%)
  local copies, waits for them, and re-layouts  9.37 us (9%)
    pallas_call x1, Pallas kernels, shards(): pl.pallas_call(kernel, out_shape=(jax.ShapeDtypeStruct(q_nope.shape, BF16...  97.8 us
    unnamed x5, local copies, waits for them, and re-layouts  7.96 us

profile of v1, /device:TPU:1, one launch (start us, length us, event | category | flops | bytes accessed | tf_op | source)
XLA Modules:
  0.0 108.6 jit_solution(11406553044052984614)
XLA Ops:
  0.6 0.9 slice.9
  1.5 0.1 reshape.11
  1.6 0.2 slice_reduce_fusion.1
  1.8 0.1 reshape_squeeze.3
  1.9 0.1 copy.23
  2.0 0.1 reshape.12
  2.1 0.1 pad_add_fusion
  2.2 0.1 select_reduce_fusion
  2.3 0.6 pad_add_fusion.1.meta
  2.9 1.4 %copy.24.k_rope = bf16[128,64]{1,0:T(8,128)(2,1)} copy(bf16[128,64]{0,1:T(8,128)(2,1)} %param.16) | data formatting | bytes 32768 | tf_op args[3]
  4.3 1.4 %copy.25.ids = s32[128,8]{1,0:T(8,128)} copy(s32[128,8]{0,1:T(8,128)} %param.21) | data formatting | bytes 8192 | tf_op args[8]
  5.7 1.4 %copy.26.weights = f32[128,8]{1,0:T(8,128)} copy(f32[128,8]{0,1:T(8,128)} %param.22) | data formatting | bytes 8192 | tf_op args[9]
  7.1 97.8 %attend_and_dispatch.1 = (bf16[128,2048]{1,0:T(8,128)(2,1)}, bf16[128,1792]{1,0:T(8,128)(2,1)}) custom-call(s32[128]{0:T(128)} %pad_add_fusion.1.meta, bf16[128,512]{1,0:T(8,128)(2,1)} %latent.1, bf16[128,64]{1,0:T(8,128)(2,1)} %copy.24.k_rope, bf16[128,1792]{1,0:T(8,128)(2,1)} %rows.1, s32[128,8]{1,0:T(8,128)} %copy.25.ids, f32[128,8]{1,0:T(8,128)} %copy.26.weights, ...), custom_call_target="tpu_custom_call" | custom-call | tf_op jit(solution)/shard_map/attend_and_dispatch/pallas_call | solution.py:557
  104.9 1.9 %copy.29 = bf16[128,2048]{1,0:T(8,128)(2,1)} copy(bf16[128,2048]{1,0:T(8,128)(2,1)} %get-tuple-element.6) | data formatting | bytes 1048576
  106.8 1.8 %copy.30 = bf16[128,1792]{1,0:T(8,128)(2,1)} copy(bf16[128,1792]{1,0:T(8,128)(2,1)} %get-tuple-element.7) | data formatting | bytes 917504
  (1 shorter events, 0.0 us)

commit v2 on v1

--- a/solution.py
+++ b/solution.py
@@ -19,6 +19,7 @@
 KW = LAT + 2 * ROPE
 RUN = 64
 GROUP = 256
+BLOCK = 512
 SCALE = 1.0 / math.sqrt(NOPE + ROPE)
 LOG2E = math.log2(math.e)
 LOW = -1e30
@@ -32,17 +33,21 @@
     return lax.dot_general(a, b, (((1,), (1,)), ((), ())), preferred_element_type=F32)
 
 
+def dot_0(a, b):
+    return lax.dot_general(a, b, (((0,), (0,)), ((), ())), preferred_element_type=F32)
+
+
 def iota(shape, dim):
     return lax.broadcasted_iota(jnp.int32, shape, dim)
 
 
 def kernel(
-    meta,
-    latent,
-    k_rope,
-    rows,
-    ids,
-    weights,
+    positions_h,
+    latent_h,
+    k_rope_h,
+    rows_h,
+    ids_h,
+    weights_h,
     q_nope_h,
     q_rope_h,
     w_uk_h,
@@ -52,13 +57,20 @@
     w_down_h,
     attn_out,
     moe_out,
+    positions,
+    latent,
+    k_rope,
+    rows,
+    ids,
+    weights,
     q_nope,
     q_rope,
     w_uk,
-    w_uv,
     w_gate,
     w_up,
     w_down,
+    index_row,
+    meta,
     outgoing,
     slots,
     to_mate,
@@ -66,14 +78,15 @@
     to_pair,
     kept,
     from_pair,
-    going,
     returned,
     keys,
     key_group,
+    value_group,
     queries,
     acc,
     row_max,
     row_sum,
+    mixed,
     load_sem,
     disp_send,
     disp_recv,
@@ -121,17 +134,22 @@
         pltpu.make_async_copy(src, dst, load_sem.at[i])
         for i, (src, dst) in enumerate(
             (
+                (ids_h, ids),
+                (weights_h, weights),
+                (rows_h, rows),
+                (k_rope_h, k_rope),
+                (latent_h, latent),
+                (positions_h, positions),
                 (q_nope_h, q_nope),
                 (q_rope_h, q_rope),
                 (w_uk_h, w_uk),
                 (w_gate_h.at[0], w_gate),
                 (w_up_h.at[0], w_up),
                 (w_down_h.at[0], w_down),
-                (w_uv_h, w_uv),
             )
         )
     ]
-    for load in loads:
+    for load in loads[:9]:
         load.start()
 
     barrier = pltpu.get_barrier_semaphore()
@@ -142,20 +160,21 @@
     pl.semaphore_signal(barrier, inc=1, device_id=(ctx, ep_pair), device_id_type=MESH)
     pl.semaphore_signal(barrier, inc=1, device_id=(ctx, ep_mate), device_id_type=MESH)
 
-    lane = iota((128, 128), 1)
+    for load in loads[:3]:
+        load.wait()
+    expert = iota((128, 128), 0)
     named = jnp.zeros((128, 128), F32)
     slot_weight = jnp.zeros((128, 128), F32)
-    for k in range(ids.shape[1]):
-        hit = (ids[:, k : k + 1] == lane) & (lane < N_CTX)
+    for k in range(ids.shape[0]):
+        hit = (ids[k : k + 1, :] == expert) & (expert < N_CTX)
         named = jnp.where(hit, 1.0, named)
-        slot_weight = jnp.where(hit, weights[:, k : k + 1], slot_weight)
-    earlier = jnp.where(lane < iota((128, 128), 0), 1.0, 0.0).astype(BF16)
-    rank = dot(earlier, named.astype(BF16))
+        slot_weight = jnp.where(hit, weights[k : k + 1, :], slot_weight)
+    earlier = jnp.where(expert < iota((128, 128), 1), 1.0, 0.0).astype(BF16)
     named_b = named.astype(BF16)
-    rank_b = rank.astype(BF16)
+    rank_b = dot(named_b, earlier).astype(BF16)
     spread = jnp.where(iota((256, 128), 0) // CAP == iota((256, 128), 1), 1.0, 0.0).astype(BF16)
-    picked = (dot_t(spread, named_b) > 0.5) & (
-        dot_t(spread, rank_b) == (iota((256, 128), 0) % CAP).astype(F32)
+    picked = (dot(spread, named_b) > 0.5) & (
+        dot(spread, rank_b) == (iota((256, 128), 0) % CAP).astype(F32)
     )
     pick = jnp.where(picked, 1.0, 0.0).astype(BF16)
     for c in range(4):
@@ -164,12 +183,17 @@
         second = dot(lhs, rows[:, half:]).reshape(8, CAP, half)
         outgoing[8 * c : 8 * (c + 1)] = jnp.concatenate([first, second], axis=1).astype(BF16)
 
-    double = jnp.where(iota((64, 128), 1) % ROPE == iota((64, 128), 0), 1.0, 0.0).astype(BF16)
+    for load in loads[3:6]:
+        load.wait()
+    double = jnp.where(iota((ROPE, 128), 1) % ROPE == iota((ROPE, 128), 0), 1.0, 0.0).astype(BF16)
     own_rows = pl.ds(pl.multiple_of(core * RUN, RUN), RUN)
     major = jnp.where(core == 0, z, y)
     minor = jnp.where(core == 0, y, z)
+    rotated = dot_0(k_rope[...], double)
     keys[core, h, major * 4 + minor, :, :LAT] = latent[own_rows, :]
-    keys[core, h, major * 4 + minor, :, LAT:] = dot(k_rope[own_rows, :], double).astype(BF16)
+    keys[core, h, major * 4 + minor, :, LAT:] = jnp.where(
+        core == 0, rotated[:RUN], rotated[RUN:]
+    ).astype(BF16)
 
     pl.semaphore_wait(barrier, 33)
 
@@ -203,22 +227,45 @@
     def wait_for(ref, sem):
         pltpu.make_async_copy(ref, ref, sem).wait()
 
-    for load in loads[:3]:
+    block = iota((N_CTX, 128), 0)
+    place_1 = N_CTX + (block // 16) * 16 + (block % 4) * 4 + (block // 4) % 4
+    held_0 = positions[:, 0:1] // RUN == iota((N_CTX, 128), 1)
+    held_1 = positions[:, RUN : RUN + 1] // RUN == iota((N_CTX, 128), 1)
+    where = jnp.sum(jnp.where(held_0, block, 0) + jnp.where(held_1, place_1, 0), axis=0)
+    index_row[...] = jnp.zeros(index_row.shape, jnp.int32)
+    index_row[0:1, :] = where.reshape(1, 128)
+    index_row[1:2, :] = positions[pl.ds(ctx, 1), :]
+    index_copy = pltpu.make_async_copy(index_row, meta, load_sem.at[0])
+    index_copy.start()
+
+    for load in loads[6:9]:
         load.wait()
-    even = iota((1, 128), 1) < ROPE
+    for load in loads[9:]:
+        load.start()
+    unit = jnp.where(iota((128, 128), 0) == iota((128, 128), 1), 1.0, 0.0).astype(BF16)
 
     @pl.loop(0, 8)
     def _(pair):
         at = pl.ds(pl.multiple_of(pair * 128, 128), 128)
-        rope = q_rope[:, at].astype(F32)
-        for which in range(2):
-            cols = pl.ds(pl.multiple_of(pair * 256 + which * 128, 128), 128)
-            lat = dot_t(q_nope[:, cols], w_uk[:, cols]).astype(BF16)
-            rot = jnp.where(even if which == 0 else ~even, rope, 0.0).astype(BF16)
-            to = pl.ds(pl.multiple_of(pair * 128 + which * 64, 64), 64)
-            for run in range(2):
-                queries[run, to, :LAT] = lat[run * 64 : (run + 1) * 64]
-                queries[run, to, LAT:] = rot[run * 64 : (run + 1) * 64]
+        cols = pl.ds(pl.multiple_of(pair * 256, 256), 256)
+        for run in range(2):
+            of_run = slice(run * RUN, (run + 1) * RUN)
+            both = q_nope[of_run, cols].astype(F32)
+            first = iota(both.shape, 1) < NOPE
+            apart = jnp.concatenate(
+                [jnp.where(first, both, 0.0), jnp.where(first, 0.0, both)], axis=0
+            ).astype(BF16)
+            queries[run, :LAT, at] = dot_t(w_uk[:, cols], apart).astype(BF16)
+            both = q_rope[of_run, at].astype(F32)
+            first = iota(both.shape, 1) < ROPE
+            apart = jnp.concatenate(
+                [jnp.where(first, both, 0.0), jnp.where(first, 0.0, both)], axis=0
+            ).astype(BF16)
+            queries[run, LAT:, at] = dot_t(unit, apart).astype(BF16)
+
+    index_copy.wait()
+    out_weights = pltpu.make_async_copy(w_uv_h, w_uk, load_sem.at[1])
+    out_weights.start()
 
     def chunk(step, dz, lo_part):
         return slots.at[lo_part * 2 + core, pl.ds(window(step) + ((z - dz + 4) % 4) * 4, 4)]
@@ -308,8 +355,9 @@
         relay(1, dz)
     for dz in (0, 1, 3, 2):
         relay_again(0, dz)
-    for load in loads[3:]:
+    for load in loads[9:]:
         load.wait()
+    wait_for(outgoing.at[pl.ds(0, 31)], disp_send.at[0])
 
     def from_experts(step):
         start = window(step)
@@ -356,95 +404,117 @@
         mine = through_down((1 - kept_lo(step)) * 2 + core)
         wait_for(from_mate.at[step, 0], back_core_recv.at[step, 0])
         to_pair[step] = (mine + from_mate[step, 0].astype(F32)).astype(BF16)
-        pltpu.make_async_remote_copy(
-            src_ref=to_pair.at[step],
-            dst_ref=from_pair.at[step],
-            send_sem=back_pair_send.at[step],
-            recv_sem=back_pair_recv.at[step],
-            device_id=(ctx, ep_pair),
-            device_id_type=MESH,
-        ).start()
+        for dz in (0, 1, 3, 2):
+            some_of = pl.ds(((z + dz) % 4) * 4, 4)
+            pltpu.make_async_remote_copy(
+                src_ref=to_pair.at[step, some_of],
+                dst_ref=from_pair.at[step, some_of],
+                send_sem=back_pair_send.at[step],
+                recv_sem=back_pair_recv.at[step, dz],
+                device_id=(ctx, ep_pair),
+                device_id_type=MESH,
+            ).start()
         mine = through_down(kept_lo(step) * 2 + core)
         wait_for(from_mate.at[step, 1], back_core_recv.at[step, 1])
         kept[step] = (mine + from_mate[step, 1].astype(F32)).astype(BF16)
 
-    def send_back(step):
-        wait_for(from_pair.at[step], back_pair_recv.at[step])
-        going[step] = (kept[step].astype(F32) + from_pair[step].astype(F32)).astype(BF16)
-        for s, dz, dy in order:
-            if s != step:
-                continue
-            to = context(s, dz, dy)
-            at = ((z + dz) % 4) * 4 + (y + dy) % 4
-            if (s, dz, dy) == (0, 0, 0):
-                pltpu.make_async_copy(going.at[0, at], returned.at[ctx], back_recv.at[0]).start()
-                continue
-            pltpu.make_async_remote_copy(
-                src_ref=going.at[s, at],
-                dst_ref=returned.at[ctx],
-                send_sem=back_send.at[0],
-                recv_sem=back_recv.at[s],
-                device_id=(to, partner_ep(s)),
-                device_id_type=MESH,
-            ).start()
-
-    run_0 = meta[64 + 2 * ctx]
-    run_1 = meta[64 + 2 * ctx + 1]
+    def send_back(step, dz):
+        start = ((z + dz) % 4) * 4
+        some_of = pl.ds(start, 4)
+        wait_for(from_pair.at[step, some_of], back_pair_recv.at[step, dz])
+        base = window(step) + start
+        outgoing[pl.ds(base, 4)] = (
+            kept[step, some_of].astype(F32) + from_pair[step, some_of].astype(F32)
+        ).astype(BF16)
+        for dy in (0, 1, 3, 2):
+            to = base + (y + dy) % 4
+
+            def send(to=to):
+                pltpu.make_async_remote_copy(
+                    src_ref=outgoing.at[to],
+                    dst_ref=returned.at[ctx],
+                    send_sem=back_send.at[0],
+                    recv_sem=back_recv.at[step],
+                    device_id=(to, partner_ep(step)),
+                    device_id_type=MESH,
+                ).start()
+
+            if step == 0 and dy == 0:
+                pl.when(dz != 0)(send)
+
+                @pl.when(dz == 0)
+                def _():
+                    pltpu.make_async_copy(
+                        outgoing.at[ctx], returned.at[ctx], back_recv.at[0]
+                    ).start()
+
+            else:
+                send()
+
+    run_0 = meta[1, 0] // RUN
+    run_1 = meta[1, RUN] // RUN
     run_late = jnp.maximum(run_0, run_1)
     run_early = jnp.minimum(run_0, run_1)
     late_half = jnp.where(run_1 > run_0, 1, 0)
     late_steps = run_late // 4 + 1
-    heads_rows = queries.shape[1]
-    blocks = heads_rows // 256
+    columns = queries.shape[2]
+
+    def take_keys(group, count):
+        for t in range(count // RUN):
+            at = jnp.clip(meta[0, group * 4 + t], 0, 2 * N_CTX - 1)
+            key_group[t * RUN : (t + 1) * RUN, :] = keys[at // 32, (at // 16) % 2, at % 16]
+        for t in range(count // 128):
+            at = slice(t * 128, (t + 1) * 128)
+            value_group[:, at] = key_group[at, :LAT].T
+
+    def attend(i, wide):
+        if wide:
+            count, group, q_half = 2 * GROUP, 2 * i, late_half
+        else:
+            is_late = i < late_steps
+            count = GROUP
+            group = jnp.where(is_late, i, i - late_steps)
+            q_half = jnp.where(is_late, late_half, 1 - late_half)
+            q_run = jnp.where(is_late, run_late, run_early)
+            turn = i == late_steps
+        take_keys(group, count)
+
+        def scores_of(b):
+            scores = dot(
+                key_group[:count, :], queries[q_half, :, b * BLOCK : (b + 1) * BLOCK]
+            )
+            if not wide:
+                key_pos = group * GROUP + iota(scores.shape, 0)
+                query_pos = q_run * RUN + iota(scores.shape, 1) % RUN
+                scores = jnp.where(key_pos <= query_pos, scores, LOW)
+            return scores
+
+        following = scores_of(0)
+        for b in range(columns // BLOCK):
+            at = slice(b * BLOCK, (b + 1) * BLOCK)
+            scores = following
+            if (b + 1) * BLOCK < columns:
+                following = scores_of(b + 1)
+            old_max = row_max[:, at]
+            if not wide:
+                old_max = jnp.where(turn, LOW, old_max)
+            new_max = jnp.maximum(old_max, jnp.max(scores, axis=0, keepdims=True))
+            fade = jnp.exp2((old_max - new_max) * (SCALE * LOG2E))
+            probs = jnp.exp2((scores - new_max[:1]) * (SCALE * LOG2E))
+            new_sum = row_sum[:, at] * fade + jnp.sum(
+                probs.reshape(count // 8, 8, BLOCK), axis=0
+            )
+            new_acc = acc[:, at] * fade[:1] + dot(value_group[:, :count], probs.astype(BF16))
+            row_max[:, at] = new_max
+            row_sum[:, at] = new_sum
+            acc[:, at] = new_acc
+            if not wide:
+                whole = jnp.sum(new_sum, axis=0, keepdims=True)
+                mixed[i - 8, :, at] = (new_acc * (1.0 / whole)).astype(BF16)
 
     row_max[...] = jnp.full(row_max.shape, LOW, F32)
     row_sum[...] = jnp.zeros(row_sum.shape, F32)
     acc[...] = jnp.zeros(acc.shape, F32)
-
-    def attend(i, kind):
-        is_late = i < late_steps
-        if kind == "late":
-            side, group, q_half, q_run = 1, i, late_half, run_late
-        elif kind == "early":
-            side, group, q_half, q_run = 0, i - late_steps, 1 - late_half, run_early
-        else:
-            side = jnp.where(is_late, 1, 0)
-            group = jnp.where(is_late, i, i - late_steps)
-            q_half = jnp.where(is_late, late_half, 1 - late_half)
-            q_run = jnp.where(is_late, run_late, run_early)
-        for t in range(4):
-            at = meta[group * 4 + t]
-            key_group[t * RUN : (t + 1) * RUN, :] = keys[at // 32, (at // 16) % 2, at % 16]
-        key_pos = group * GROUP + iota((256, 256), 1)
-        query_pos = q_run * RUN + iota((256, 256), 0) % RUN
-        for b in range(blocks):
-            at = slice(b * 256, (b + 1) * 256)
-            scores = dot_t(queries[q_half, at, :], key_group[...])
-            if masked(kind):
-                scores = jnp.where(key_pos <= query_pos, scores, LOW)
-            old_max = row_max[side, at, :]
-            new_max = jnp.maximum(old_max, jnp.max(scores, axis=1, keepdims=True))
-            fade = jnp.exp2((old_max - new_max) * (SCALE * LOG2E))
-            probs = jnp.exp2(
-                (scores - jnp.concatenate([new_max, new_max], axis=1)) * (SCALE * LOG2E)
-            )
-            new_sum = row_sum[side, at, :] * fade + (probs[:, :128] + probs[:, 128:])
-            new_acc = acc[side, at, :] * jnp.concatenate([fade] * 4, axis=1) + dot(
-                probs.astype(BF16), key_group[:, :LAT]
-            )
-            if kind == "any":
-                for to in range(2):
-                    here = side == to
-                    row_max[to, at, :] = jnp.where(here, new_max, row_max[to, at, :])
-                    row_sum[to, at, :] = jnp.where(here, new_sum, row_sum[to, at, :])
-                    acc[to, at, :] = jnp.where(here, new_acc, acc[to, at, :])
-            else:
-                row_max[side, at, :] = new_max
-                row_sum[side, at, :] = new_sum
-                acc[side, at, :] = new_acc
-
-    def masked(kind):
-        return kind != "late"
 
     from_experts(0)
     for dz in (0, 1, 3, 2):
@@ -455,50 +525,47 @@
     keys_share(2)
     wait_for(keys.at[1 - core], ag_recv.at[5])
 
+    def gray(i):
+        return jnp.where(i < 2, i, 5 - i)
+
     @pl.loop(0, 4)
     def _(i):
-        attend(i, "late")
-
-    send_back(0)
-
-    @pl.loop(4, 8)
+        attend(i, True)
+        send_back(0, gray(i))
+
+    @pl.loop(0, 4)
     def _(i):
-        attend(i, "late")
-
-    @pl.loop(8, 12)
-    def _(i):
-        attend(i, "any")
-
-    send_back(1)
-
-    @pl.loop(12, 16)
-    def _(i):
-        attend(i, "any")
-
-    attend(jnp.int32(16), "early")
-
-    first_side = jnp.where(run_0 > run_1, 1, 0)
-
-    @pl.loop(0, 16)
-    def _(head):
-        at = pl.ds(pl.multiple_of(head * 64, 64), 64)
-        cols = pl.ds(pl.multiple_of(head * 128, 128), 128)
-        both = []
-        for side in (first_side, 1 - first_side):
-            total = jnp.sum(row_sum[side, at, :], axis=1, keepdims=True)
-            both.append(acc[side, at, :] / total)
-        mixed = jnp.concatenate(both, axis=0).astype(BF16)
-        attn_out[:, cols] = dot(mixed, w_uv[:, cols]).astype(BF16)
+        attend(8 + 2 * i, False)
+        attend(9 + 2 * i, False)
+        send_back(1, gray(i))
+
+    attend(jnp.int32(16), False)
+
+    out_weights.wait()
+    late_at = jnp.clip(late_steps - 9, 0, 7)
+
+    @pl.loop(0, 8)
+    def _(pair):
+        at = pl.ds(pl.multiple_of(pair * 128, 128), 128)
+        for run in range(2):
+            place = jnp.where(late_half == run, late_at, 8)
+            cols = pl.ds(pl.multiple_of(pair * 256, 256), 256)
+            both = dot_0(mixed[place, :, at], w_uk[:, cols])
+            for i in range(2):
+                to = pl.ds(pl.multiple_of(pair * 256 + i * 128, 128), 128)
+                attn_out[run * RUN : (run + 1) * RUN, to] = both[
+                    i * RUN : (i + 1) * RUN, i * 128 : (i + 1) * 128
+                ].astype(BF16)
 
     wide = (128, N_CTX * 2 * CAP)
     column = iota(wide, 1)
     spread_2 = jnp.where(column // (2 * CAP) == iota(wide, 0), 1.0, 0.0).astype(BF16)
     weight_hi = slot_weight.astype(BF16)
     weight_lo = (slot_weight - weight_hi.astype(F32)).astype(BF16)
-    here = (dot(named_b, spread_2) > 0.5) & (
-        dot(rank_b, spread_2) == (column % CAP).astype(F32)
+    here = (dot_0(named_b, spread_2) > 0.5) & (
+        dot_0(rank_b, spread_2) == (column % CAP).astype(F32)
     )
-    parts = [dot(w, spread_2) for w in (weight_hi, weight_lo)]
+    parts = [dot_0(w, spread_2) for w in (weight_hi, weight_lo)]
     wait_for(returned.at[pl.ds(0, 16)], back_recv.at[0])
     wait_for(returned.at[pl.ds(0, 16)], back_recv.at[1])
     for i in range(2):
@@ -509,7 +576,6 @@
             total = total + dot(factor, returned[...].reshape(N_CTX * 2 * CAP, half))
         moe_out[:, i * half : (i + 1) * half] = total.astype(BF16)
 
-    wait_for(outgoing.at[pl.ds(0, 31)], disp_send.at[0])
     wait_for(slots.at[0], pair_send.at[0])
     wait_for(slots.at[pl.ds(0, 2)], core_send.at[0])
     wait_for(keys.at[0, 0, 0], ag_send.at[0])
@@ -538,21 +604,12 @@
     w_up,
     w_down,
 ):
-    runs = positions[::RUN] // RUN
-    pairs = runs.reshape(N_CTX, 2)
-    placed = jnp.concatenate(
-        [pairs[:, 0], pairs[:, 1].reshape(2, 4, 4).transpose(0, 2, 1).reshape(N_CTX)]
-    )
-    spots = jnp.arange(2 * N_CTX, dtype=jnp.int32)
-    where = jnp.sum(jnp.where(placed[None, :] == spots[:, None], spots[None, :], 0), axis=1)
-    meta = jnp.concatenate([where, runs]).astype(jnp.int32)
-
     count, part = moe_rows.shape
     half = part // 2
     vmem = pl.BlockSpec(memory_space=pltpu.VMEM)
     anywhere = pl.BlockSpec(memory_space=pl.ANY)
     dma = pltpu.SemaphoreType.DMA
-    heads_rows = q_nope.shape[1] // NOPE * RUN
+    columns = q_nope.shape[1] // NOPE * RUN
     slot = (2 * CAP, half)
     return pl.pallas_call(
         kernel,
@@ -560,16 +617,23 @@
             jax.ShapeDtypeStruct(q_nope.shape, BF16),
             jax.ShapeDtypeStruct(moe_rows.shape, BF16),
         ),
-        in_specs=[pl.BlockSpec(memory_space=pltpu.SMEM)] + [vmem] * 5 + [anywhere] * 7,
+        in_specs=[anywhere] * 13,
         out_specs=(vmem, vmem),
         scratch_shapes=[
+            pltpu.VMEM((N_CTX, count), jnp.int32),
+            pltpu.VMEM(latent.shape, BF16),
+            pltpu.VMEM(k_rope.shape[::-1], BF16),
+            pltpu.VMEM(moe_rows.shape, BF16),
+            pltpu.VMEM(expert_ids.shape[::-1], jnp.int32),
+            pltpu.VMEM(expert_weights.shape[::-1], F32),
             pltpu.VMEM(q_nope.shape, BF16),
             pltpu.VMEM(q_rope.shape, BF16),
             pltpu.VMEM(w_uk.shape, BF16),
-            pltpu.VMEM(w_uv.shape, BF16),
             pltpu.VMEM(w_gate.shape[1:], BF16),
             pltpu.VMEM(w_up.shape[1:], BF16),
             pltpu.VMEM(w_down.shape[1:], BF16),
+            pltpu.VMEM((8, 128), jnp.int32),
+            pltpu.SMEM((8, 128), jnp.int32),
             pltpu.VMEM((N_CTX,) + slot, BF16),
             pltpu.VMEM((4, N_CTX) + slot, BF16),
             pltpu.VMEM((2, 2, 16) + slot, BF16),
@@ -577,15 +641,16 @@
             pltpu.VMEM((2, 16) + slot, BF16),
             pltpu.VMEM((2, 16) + slot, BF16),
             pltpu.VMEM((2, 16) + slot, BF16),
-            pltpu.VMEM((2, 16) + slot, BF16),
             pltpu.VMEM((N_CTX,) + slot, BF16),
             pltpu.VMEM((2, 2, 16, RUN, KW), BF16),
-            pltpu.VMEM((GROUP, KW), BF16),
-            pltpu.VMEM((2, heads_rows, KW), BF16),
-            pltpu.VMEM((2, heads_rows, LAT), F32),
-            pltpu.VMEM((2, heads_rows, 128), F32),
-            pltpu.VMEM((2, heads_rows, 128), F32),
-            dma((7,)),
+            pltpu.VMEM((2 * GROUP, KW), BF16),
+            pltpu.VMEM((LAT, 2 * GROUP), BF16),
+            pltpu.VMEM((2, KW, columns), BF16),
+            pltpu.VMEM((LAT, columns), F32),
+            pltpu.VMEM((8, columns), F32),
+            pltpu.VMEM((8, columns), F32),
+            pltpu.VMEM((9, LAT, columns), BF16),
+            dma((12,)),
             dma((1,)),
             dma((2, 4)),
             dma((1,)),
@@ -597,7 +662,7 @@
             dma((2, 2)),
             dma((2, 2)),
             dma((2,)),
-            dma((2,)),
+            dma((2, 4)),
             dma((1,)),
             dma((2,)),
         ],
@@ -606,12 +671,12 @@
         ),
         name="attend_and_dispatch",
     )(
-        meta,
+        positions.reshape(N_CTX, count),
         latent,
-        k_rope,
+        k_rope.T,
         moe_rows,
-        expert_ids,
-        expert_weights,
+        expert_ids.T,
+        expert_weights.T,
         q_nope,
         q_rope,
         w_uk,

time: 109 us -> 81.9 us (0.75)
  Pallas kernels: 97.8 us -> 77.4 us
  local copies, waits for them, and re-layouts: 9.37 us -> 3.7 us
    pallas_call x1, Pallas kernels: 97.8 us -> 77.4 us  [shards(): pl.pallas_call(kernel, out_shape=(jax.ShapeDtypeStruct(q_nope.shape, BF16...]
    unnamed x5 -> x2, local copies, waits for them, and re-layouts: 7.96 us -> 3.7 us
where the time goes in v2:
time: 81.9 us; the launch traced here: 81.7 us
  Pallas kernels  77.4 us (95%)
  local copies, waits for them, and re-layouts  3.7 us (5%)
    pallas_call x1, Pallas kernels, shards(): pl.pallas_call(kernel, out_shape=(jax.ShapeDtypeStruct(q_nope.shape, BF16...  77.4 us
    unnamed x2, local copies, waits for them, and re-layouts  3.7 us

profile of v2, /device:TPU:1, one launch (start us, length us, event | category | flops | bytes accessed | tf_op | source)
XLA Modules:
  0.0 81.7 jit_solution(5264891868955353345)
XLA Ops:
  0.6 77.4 %attend_and_dispatch.1 = (bf16[128,2048]{1,0:T(8,128)(2,1)}, bf16[128,1792]{1,0:T(8,128)(2,1)}) custom-call(s32[32,128]{1,0:T(8,128)} %bitcast.4, bf16[128,512]{1,0:T(8,128)(2,1)} %latent_h.1, bf16[64,128]{1,0:T(8,128)(2,1)} %bitcast.5, bf16[128,1792]{1,0:T(8,128)(2,1)} %rows_h.1, s32[8,128]{1,0:T(8,128)} %bitcast.6, f32[8,128]{1,0:T(8,128)} %bitcast.7, ...), custom_call_target="tpu_custom_call" | custom-call | tf_op jit(solution)/shard_map/attend_and_dispatch/pallas_call | solution.py:614
  78.0 1.9 %copy.17 = bf16[128,2048]{1,0:T(8,128)(2,1)} copy(bf16[128,2048]{1,0:T(8,128)(2,1)} %get-tuple-element.4) | data formatting | bytes 1048576
  79.9 1.8 %copy.18 = bf16[128,1792]{1,0:T(8,128)(2,1)} copy(bf16[128,1792]{1,0:T(8,128)(2,1)} %get-tuple-element.5) | data formatting | bytes 917504

commit v3 on v2

--- a/solution.py
+++ b/solution.py
@@ -18,6 +18,7 @@
 N_CTX = 32
 KW = LAT + 2 * ROPE
 RUN = 64
+PIECE = 32
 GROUP = 256
 BLOCK = 512
 SCALE = 1.0 / math.sqrt(NOPE + ROPE)
@@ -186,14 +187,14 @@
     for load in loads[3:6]:
         load.wait()
     double = jnp.where(iota((ROPE, 128), 1) % ROPE == iota((ROPE, 128), 0), 1.0, 0.0).astype(BF16)
-    own_rows = pl.ds(pl.multiple_of(core * RUN, RUN), RUN)
-    major = jnp.where(core == 0, z, y)
-    minor = jnp.where(core == 0, y, z)
+    majors, minors = (z, y), (y, z)
+    own_place = [majors[f] * 4 + minors[f] for f in range(2)]
     rotated = dot_0(k_rope[...], double)
-    keys[core, h, major * 4 + minor, :, :LAT] = latent[own_rows, :]
-    keys[core, h, major * 4 + minor, :, LAT:] = jnp.where(
-        core == 0, rotated[:RUN], rotated[RUN:]
-    ).astype(BF16)
+    rotated = jnp.where(core == 0, rotated[:RUN], rotated[RUN:]).astype(BF16)
+    for f in range(2):
+        own_rows = pl.ds(pl.multiple_of(core * RUN + f * PIECE, PIECE), PIECE)
+        keys[core, f, h, own_place[f], :, :LAT] = latent[own_rows, :]
+        keys[core, f, h, own_place[f], :, LAT:] = rotated[f * PIECE : (f + 1) * PIECE]
 
     pl.semaphore_wait(barrier, 33)
 
@@ -210,28 +211,62 @@
             device_id_type=MESH,
         ).start()
 
-    def at_axis(major_to, minor_to):
-        z_to = jnp.where(core == 0, major_to, minor_to)
-        y_to = jnp.where(core == 0, minor_to, major_to)
-        return h * 16 + z_to * 4 + y_to
-
-    pltpu.make_async_remote_copy(
-        src_ref=keys.at[core, h, major * 4 + minor],
-        dst_ref=keys.at[core, h, major * 4 + minor],
-        send_sem=ag_send.at[0],
-        recv_sem=ag_recv.at[0],
-        device_id=((1 - h) * 16 + z * 4 + y, ep_pair),
-        device_id_type=MESH,
-    ).start()
+    def at_axis(f, major_to, minor_to):
+        return h * 16 + (major_to * 4 + minor_to if f == 0 else minor_to * 4 + major_to)
+
+    def send_keys(region, sent, arrived, to):
+        pltpu.make_async_remote_copy(
+            src_ref=region,
+            dst_ref=region,
+            send_sem=ag_send.at[sent],
+            recv_sem=ag_recv.at[arrived],
+            device_id=to,
+            device_id_type=MESH,
+        ).start()
+
+    def keys_first():
+        for f in range(2):
+            send_keys(keys.at[core, f, h, own_place[f]], 0, 0, ((1 - h) * 16 + z * 4 + y, ep_pair))
+
+    def keys_second(which):
+        side = h if which == 0 else 1 - h
+        if which == 1:
+            wait_for(keys.at[core, :, side, 0], ag_recv.at[0])
+        for t in (1, 3, 2):
+            for f in range(2):
+                to = (at_axis(f, majors[f], (minors[f] + t) % 4), ep)
+                send_keys(keys.at[core, f, side, own_place[f]], 1, 1 + which, to)
+
+    def keys_third(which):
+        side = h if which == 0 else 1 - h
+        wait_for(keys.at[core, :, side, pl.ds(0, 3)], ag_recv.at[1 + which])
+        for t in (1, 3, 2):
+            for f in range(2):
+                to = (at_axis(f, (majors[f] + t) % 4, minors[f]), ep)
+                region = keys.at[core, f, side, pl.ds(majors[f] * 4, 4)]
+                send_keys(region, 2, 2 + 3 * which + t, to)
+        for f in range(2):
+            region = keys.at[core, f, side, pl.ds(majors[f] * 4, 4)]
+            send_keys(region, 3, 9, (ctx, ep_mate))
+
+    def keys_share(which, t):
+        side = h if which == 0 else 1 - h
+        wait_for(keys.at[core, :, side, pl.ds(0, 4)], ag_recv.at[2 + 3 * which + t])
+        for f in range(2):
+            at = (majors[f] - t + 4) % 4
+            send_keys(keys.at[core, f, side, pl.ds(at * 4, 4)], 3, 9, (ctx, ep_mate))
 
     def wait_for(ref, sem):
         pltpu.make_async_copy(ref, ref, sem).wait()
 
+    keys_first()
+
     block = iota((N_CTX, 128), 0)
-    place_1 = N_CTX + (block // 16) * 16 + (block % 4) * 4 + (block // 4) % 4
     held_0 = positions[:, 0:1] // RUN == iota((N_CTX, 128), 1)
     held_1 = positions[:, RUN : RUN + 1] // RUN == iota((N_CTX, 128), 1)
-    where = jnp.sum(jnp.where(held_0, block, 0) + jnp.where(held_1, place_1, 0), axis=0)
+    where = jnp.sum(
+        jnp.where(held_0, 2 * block, 0) + jnp.where(held_1, 2 * block + 1, 0), axis=0
+    )
     index_row[...] = jnp.zeros(index_row.shape, jnp.int32)
     index_row[0:1, :] = where.reshape(1, 128)
     index_row[1:2, :] = positions[pl.ds(ctx, 1), :]
@@ -301,63 +336,6 @@
             device_id=(ctx, ep_mate),
             device_id_type=MESH,
         ).start()
-
-    def keys_second():
-        wait_for(keys.at[core, 1 - h, major * 4 + minor], ag_recv.at[0])
-        for t in (1, 3, 2):
-            region = keys.at[core, :, major * 4 + minor]
-            pltpu.make_async_remote_copy(
-                src_ref=region,
-                dst_ref=region,
-                send_sem=ag_send.at[1],
-                recv_sem=ag_recv.at[1],
-                device_id=(at_axis(major, (minor + t) % 4), ep),
-                device_id_type=MESH,
-            ).start()
-
-    def keys_to_mate(at):
-        region = keys.at[core, :, pl.ds(at * 4, 4)]
-        pltpu.make_async_remote_copy(
-            src_ref=region,
-            dst_ref=region,
-            send_sem=ag_send.at[3],
-            recv_sem=ag_recv.at[5],
-            device_id=(ctx, ep_mate),
-            device_id_type=MESH,
-        ).start()
-
-    def keys_third():
-        wait_for(keys.at[core, :, pl.ds(0, 3)], ag_recv.at[1])
-        region = keys.at[core, :, pl.ds(major * 4, 4)]
-        for t in (1, 3, 2):
-            pltpu.make_async_remote_copy(
-                src_ref=region,
-                dst_ref=region,
-                send_sem=ag_send.at[2],
-                recv_sem=ag_recv.at[1 + t],
-                device_id=(at_axis((major + t) % 4, minor), ep),
-                device_id_type=MESH,
-            ).start()
-        keys_to_mate(major)
-
-    def keys_share(t):
-        at = (major - t + 4) % 4
-        wait_for(keys.at[core, :, pl.ds(at * 4, 4)], ag_recv.at[1 + t])
-        keys_to_mate(at)
-
-    relay(0, 0)
-    keys_second()
-    relay(0, 1)
-    relay(0, 3)
-    relay(0, 2)
-    keys_third()
-    for dz in (0, 1, 3, 2):
-        relay(1, dz)
-    for dz in (0, 1, 3, 2):
-        relay_again(0, dz)
-    for load in loads[9:]:
-        load.wait()
-    wait_for(outgoing.at[pl.ds(0, 31)], disp_send.at[0])
 
     def from_experts(step):
         start = window(step)
@@ -462,7 +440,11 @@
     def take_keys(group, count):
         for t in range(count // RUN):
             at = jnp.clip(meta[0, group * 4 + t], 0, 2 * N_CTX - 1)
-            key_group[t * RUN : (t + 1) * RUN, :] = keys[at // 32, (at // 16) % 2, at % 16]
+            of, c = at % 2, at // 2
+            z_at, y_at = (c // 4) % 4, c % 4
+            first, second = t * RUN, t * RUN + PIECE
+            key_group[first:second, :] = keys[of, 0, c // 16, z_at * 4 + y_at]
+            key_group[second : second + PIECE, :] = keys[of, 1, c // 16, y_at * 4 + z_at]
         for t in range(count // 128):
             at = slice(t * 128, (t + 1) * 128)
             value_group[:, at] = key_group[at, :LAT].T
@@ -516,17 +498,41 @@
     row_sum[...] = jnp.zeros(row_sum.shape, F32)
     acc[...] = jnp.zeros(acc.shape, F32)
 
-    from_experts(0)
-    for dz in (0, 1, 3, 2):
-        relay_again(1, dz)
-    from_experts(1)
-    keys_share(1)
-    keys_share(3)
-    keys_share(2)
-    wait_for(keys.at[1 - core], ag_recv.at[5])
-
     def gray(i):
         return jnp.where(i < 2, i, 5 - i)
+
+    relay(0, 0)
+    keys_second(0)
+    relay(0, 1)
+    keys_second(1)
+    relay(0, 3)
+    relay(0, 2)
+    relay(1, 0)
+    keys_third(0)
+    relay(1, 1)
+    keys_third(1)
+    relay(1, 3)
+    relay(1, 2)
+    relay_again(0, 0)
+    relay_again(0, 1)
+    relay_again(0, 3)
+    relay_again(0, 2)
+    for load in loads[9:]:
+        load.wait()
+    wait_for(outgoing.at[pl.ds(0, 31)], disp_send.at[0])
+    from_experts(0)
+    keys_share(0, 1)
+    relay_again(1, 0)
+    keys_share(0, 3)
+    relay_again(1, 1)
+    keys_share(0, 2)
+    relay_again(1, 3)
+    relay_again(1, 2)
+    from_experts(1)
+    keys_share(1, 1)
+    keys_share(1, 3)
+    keys_share(1, 2)
+    wait_for(keys.at[1 - core], ag_recv.at[9])
 
     @pl.loop(0, 4)
     def _(i):
@@ -578,9 +584,9 @@
 
     wait_for(slots.at[0], pair_send.at[0])
     wait_for(slots.at[pl.ds(0, 2)], core_send.at[0])
-    wait_for(keys.at[0, 0, 0], ag_send.at[0])
-    wait_for(keys.at[0, :, pl.ds(0, 3)], ag_send.at[1])
-    wait_for(keys.at[0, :, pl.ds(0, 12)], ag_send.at[2])
+    wait_for(keys.at[0, :, 0, 0], ag_send.at[0])
+    wait_for(keys.at[0, 0, 0, pl.ds(0, 12)], ag_send.at[1])
+    wait_for(keys.at[0, :, :, pl.ds(0, 12)], ag_send.at[2])
     wait_for(keys.at[0], ag_send.at[3])
     for step in range(2):
         for j in range(2):
@@ -642,7 +648,7 @@
             pltpu.VMEM((2, 16) + slot, BF16),
             pltpu.VMEM((2, 16) + slot, BF16),
             pltpu.VMEM((N_CTX,) + slot, BF16),
-            pltpu.VMEM((2, 2, 16, RUN, KW), BF16),
+            pltpu.VMEM((2, 2, 2, 16, PIECE, KW), BF16),
             pltpu.VMEM((2 * GROUP, KW), BF16),
             pltpu.VMEM((LAT, 2 * GROUP), BF16),
             pltpu.VMEM((2, KW, columns), BF16),
@@ -658,7 +664,7 @@
             dma((1,)),
             dma((2, 2)),
             dma((4,)),
-            dma((6,)),
+            dma((10,)),
             dma((2, 2)),
             dma((2, 2)),
             dma((2,)),

time: 81.9 us -> 77.7 us (0.949); the launches traced: 81.7 us -> 76.7 us
  Pallas kernels: 77.4 us -> 72.3 us
    pallas_call x1, Pallas kernels: 77.4 us -> 72.3 us  [shards(): pl.pallas_call(kernel, out_shape=(jax.ShapeDtypeStruct(q_nope.shape, BF16...]
where the time goes in v3:
time: 77.7 us; the launch traced here: 76.7 us
  Pallas kernels  72.3 us (93%)
  local copies, waits for them, and re-layouts  3.7 us (5%)
    pallas_call x1, Pallas kernels, shards(): pl.pallas_call(kernel, out_shape=(jax.ShapeDtypeStruct(q_nope.shape, BF16...  72.3 us
    unnamed x2, local copies, waits for them, and re-layouts  3.7 us

profile of v3, /device:TPU:1, one launch (start us, length us, event | category | flops | bytes accessed | tf_op | source)
XLA Modules:
  0.0 76.7 jit_solution(10159958393529189629)
XLA Ops:
  0.6 72.3 %attend_and_dispatch.1 = (bf16[128,2048]{1,0:T(8,128)(2,1)}, bf16[128,1792]{1,0:T(8,128)(2,1)}) custom-call(s32[32,128]{1,0:T(8,128)} %bitcast.4, bf16[128,512]{1,0:T(8,128)(2,1)} %latent_h.1, bf16[64,128]{1,0:T(8,128)(2,1)} %bitcast.5, bf16[128,1792]{1,0:T(8,128)(2,1)} %rows_h.1, s32[8,128]{1,0:T(8,128)} %bitcast.6, f32[8,128]{1,0:T(8,128)} %bitcast.7, ...), custom_call_target="tpu_custom_call" | custom-call | tf_op jit(solution)/shard_map/attend_and_dispatch/pallas_call | solution.py:620
  73.0 1.9 %copy.17 = bf16[128,2048]{1,0:T(8,128)(2,1)} copy(bf16[128,2048]{1,0:T(8,128)(2,1)} %get-tuple-element.4) | data formatting | bytes 1048576
  74.8 1.8 %copy.18 = bf16[128,1792]{1,0:T(8,128)(2,1)} copy(bf16[128,1792]{1,0:T(8,128)(2,1)} %get-tuple-element.5) | data formatting | bytes 917504

commit v4 on v3

--- a/solution.py
+++ b/solution.py
@@ -254,7 +254,7 @@
         wait_for(keys.at[core, :, side, pl.ds(0, 4)], ag_recv.at[2 + 3 * which + t])
         for f in range(2):
             at = (majors[f] - t + 4) % 4
-            send_keys(keys.at[core, f, side, pl.ds(at * 4, 4)], 3, 9, (ctx, ep_mate))
+            send_keys(keys.at[core, f, side, pl.ds(at * 4, 4)], 3, 9 + t, (ctx, ep_mate))
 
     def wait_for(ref, sem):
         pltpu.make_async_copy(ref, ref, sem).wait()
@@ -270,6 +270,9 @@
     index_row[...] = jnp.zeros(index_row.shape, jnp.int32)
     index_row[0:1, :] = where.reshape(1, 128)
     index_row[1:2, :] = positions[pl.ds(ctx, 1), :]
+    swapped = jnp.where(positions[:, 0:1] > positions[:, RUN : RUN + 1], 1, 0)
+    swapped = jnp.sum(jnp.where(block == iota((N_CTX, 128), 1), swapped, 0), axis=0)
+    index_row[2:3, :] = swapped.reshape(1, 128)
     index_copy = pltpu.make_async_copy(index_row, meta, load_sem.at[0])
     index_copy.start()
 
@@ -437,6 +440,23 @@
     late_steps = run_late // 4 + 1
     columns = queries.shape[2]
 
+    def take_values(count):
+        for t in range(count // 128):
+            at = slice(t * 128, (t + 1) * 128)
+            value_group[:, at] = key_group[at, :LAT].T
+
+    def take_early(t):
+        for f in range(2):
+            row = (majors[f] - t + 4) % 4
+            for n in range(8):
+                side, a = n // 4, n % 4
+                c = side * 16 + (row * 4 + a if f == 0 else a * 4 + row)
+                to = (f * 8 + n) * PIECE
+                key_group[to : to + PIECE, :] = jnp.where(
+                    meta[2, c] == 1, keys[1, f, side, row * 4 + a], keys[0, f, side, row * 4 + a]
+                )
+        take_values(2 * GROUP)
+
     def take_keys(group, count):
         for t in range(count // RUN):
             at = jnp.clip(meta[0, group * 4 + t], 0, 2 * N_CTX - 1)
@@ -445,13 +465,12 @@
             first, second = t * RUN, t * RUN + PIECE
             key_group[first:second, :] = keys[of, 0, c // 16, z_at * 4 + y_at]
             key_group[second : second + PIECE, :] = keys[of, 1, c // 16, y_at * 4 + z_at]
-        for t in range(count // 128):
-            at = slice(t * 128, (t + 1) * 128)
-            value_group[:, at] = key_group[at, :LAT].T
+        take_values(count)
 
     def attend(i, wide):
         if wide:
-            count, group, q_half = 2 * GROUP, 2 * i, late_half
+            count, q_half = 2 * GROUP, late_half
+            take_early(i)
         else:
             is_late = i < late_steps
             count = GROUP
@@ -459,7 +478,7 @@
             q_half = jnp.where(is_late, late_half, 1 - late_half)
             q_run = jnp.where(is_late, run_late, run_early)
             turn = i == late_steps
-        take_keys(group, count)
+            take_keys(group, count)
 
         def scores_of(b):
             scores = dot(
@@ -500,6 +519,10 @@
 
     def gray(i):
         return jnp.where(i < 2, i, 5 - i)
+
+    def attend_early(t):
+        wait_for(keys.at[1 - core, :, :, pl.ds(0, 4)], ag_recv.at[9 + t])
+        attend(t, True)
 
     relay(0, 0)
     keys_second(0)
@@ -530,14 +553,16 @@
     relay_again(1, 2)
     from_experts(1)
     keys_share(1, 1)
+    attend_early(0)
+    send_back(0, 0)
     keys_share(1, 3)
+    attend_early(1)
+    send_back(0, 1)
     keys_share(1, 2)
-    wait_for(keys.at[1 - core], ag_recv.at[9])
-
-    @pl.loop(0, 4)
-    def _(i):
-        attend(i, True)
-        send_back(0, gray(i))
+    attend_early(3)
+    send_back(0, 3)
+    attend_early(2)
+    send_back(0, 2)
 
     @pl.loop(0, 4)
     def _(i):
@@ -593,6 +618,11 @@
             wait_for(to_mate.at[step, j], back_core_send.at[step, j])
         wait_for(to_pair.at[step], back_pair_send.at[step])
     wait_for(outgoing.at[pl.ds(0, 31)], back_send.at[0])
+
+
+def hand_over(attn, moe, attn_out, moe_out):
+    attn_out[...] = attn[...]
+    moe_out[...] = moe[...]
 
 
 def shards(
@@ -617,7 +647,7 @@
     dma = pltpu.SemaphoreType.DMA
     columns = q_nope.shape[1] // NOPE * RUN
     slot = (2 * CAP, half)
-    return pl.pallas_call(
+    results = pl.pallas_call(
         kernel,
         out_shape=(
             jax.ShapeDtypeStruct(q_nope.shape, BF16),
@@ -664,7 +694,7 @@
             dma((1,)),
             dma((2, 2)),
             dma((4,)),
-            dma((10,)),
+            dma((13,)),
             dma((2, 2)),
             dma((2, 2)),
             dma((2,)),
@@ -691,6 +721,13 @@
         w_up,
         w_down,
     )
+    return pl.pallas_call(
+        hand_over,
+        out_shape=tuple(jax.ShapeDtypeStruct(r.shape, r.dtype) for r in results),
+        in_specs=[vmem] * 2,
+        out_specs=(vmem, vmem),
+        name="hand_over",
+    )(*results)
 
 
 def solution(mesh):

time: 77.7 us -> 74 us (0.952)
  local copies, waits for them, and re-layouts: 3.7 us -> 0 us
    unnamed x2 -> x0, local copies, waits for them, and re-layouts: 3.7 us -> none
    pallas_call x1, Pallas kernels: 72.3 us -> 69.9 us  [shards(): pl.pallas_call(kernel, out_shape=(jax.ShapeDtypeStruct(q_nope.shape, BF16...]
    pallas_call x0 -> x1, Pallas kernels: none -> 2.15 us  [shards(): pl.pallas_call(hand_over, out_shape=tuple((jax.ShapeDtypeStruct(r.shape,...]
where the time goes in v4:
time: 74 us; the launch traced here: 72.7 us
  Pallas kernels  72 us (97%)
    pallas_call x1, Pallas kernels, shards(): pl.pallas_call(kernel, out_shape=(jax.ShapeDtypeStruct(q_nope.shape, BF16...  69.9 us
    pallas_call x1, Pallas kernels, shards(): pl.pallas_call(hand_over, out_shape=tuple((jax.ShapeDtypeStruct(r.shape,...  2.15 us

profile of v4, /device:TPU:1, one launch (start us, length us, event | category | flops | bytes accessed | tf_op | source)
XLA Modules:
  0.0 72.7 jit_solution(7040273716904726518)
XLA Ops:
  0.6 69.9 %attend_and_dispatch.1 = (bf16[128,2048]{1,0:T(8,128)(2,1)}, bf16[128,1792]{1,0:T(8,128)(2,1)}) custom-call(s32[32,128]{1,0:T(8,128)} %bitcast.4, bf16[128,512]{1,0:T(8,128)(2,1)} %latent_h.1, bf16[64,128]{1,0:T(8,128)(2,1)} %bitcast.5, bf16[128,1792]{1,0:T(8,128)(2,1)} %rows_h.1, s32[8,128]{1,0:T(8,128)} %bitcast.6, f32[8,128]{1,0:T(8,128)} %bitcast.7, ...), custom_call_target="tpu_custom_call" | custom-call | tf_op jit(solution)/shard_map/attend_and_dispatch/pallas_call | solution.py:650
  70.5 2.2 %hand_over.1 = (bf16[128,2048]{1,0:T(8,128)(2,1)}, bf16[128,1792]{1,0:T(8,128)(2,1)}) custom-call(bf16[128,2048]{1,0:T(8,128)(2,1)} %get-tuple-element.4.attn, bf16[128,1792]{1,0:T(8,128)(2,1)} %get-tuple-element.5.moe), custom_call_target="tpu_custom_call" | custom-call | tf_op jit(solution)/shard_map/hand_over/pallas_call | solution.py:724

commit v5 on v4

--- a/solution.py
+++ b/solution.py
@@ -340,6 +340,17 @@
             device_id_type=MESH,
         ).start()
 
+    def send_sums(step, dz):
+        some_of = pl.ds(((z + dz) % 4) * 4, 4)
+        pltpu.make_async_remote_copy(
+            src_ref=to_pair.at[step, some_of],
+            dst_ref=from_pair.at[step, some_of],
+            send_sem=back_pair_send.at[step],
+            recv_sem=back_pair_recv.at[step, dz],
+            device_id=(ctx, ep_pair),
+            device_id_type=MESH,
+        ).start()
+
     def from_experts(step):
         start = window(step)
         for j in range(2):
@@ -385,16 +396,8 @@
         mine = through_down((1 - kept_lo(step)) * 2 + core)
         wait_for(from_mate.at[step, 0], back_core_recv.at[step, 0])
         to_pair[step] = (mine + from_mate[step, 0].astype(F32)).astype(BF16)
-        for dz in (0, 1, 3, 2):
-            some_of = pl.ds(((z + dz) % 4) * 4, 4)
-            pltpu.make_async_remote_copy(
-                src_ref=to_pair.at[step, some_of],
-                dst_ref=from_pair.at[step, some_of],
-                send_sem=back_pair_send.at[step],
-                recv_sem=back_pair_recv.at[step, dz],
-                device_id=(ctx, ep_pair),
-                device_id_type=MESH,
-            ).start()
+        for dz in (0, 1, 3, 2) if step == 0 else (0, 1):
+            send_sums(step, dz)
         mine = through_down(kept_lo(step) * 2 + core)
         wait_for(from_mate.at[step, 1], back_core_recv.at[step, 1])
         kept[step] = (mine + from_mate[step, 1].astype(F32)).astype(BF16)
@@ -555,22 +558,27 @@
     keys_share(1, 1)
     attend_early(0)
     send_back(0, 0)
+    send_back(0, 1)
+    send_sums(1, 3)
     keys_share(1, 3)
     attend_early(1)
-    send_back(0, 1)
+    send_back(0, 3)
+    send_sums(1, 2)
+    send_back(0, 2)
     keys_share(1, 2)
     attend_early(3)
-    send_back(0, 3)
     attend_early(2)
-    send_back(0, 2)
-
-    @pl.loop(0, 4)
+    send_back(1, 0)
+
+    @pl.loop(0, 3)
     def _(i):
         attend(8 + 2 * i, False)
         attend(9 + 2 * i, False)
-        send_back(1, gray(i))
-
-    attend(jnp.int32(16), False)
+        send_back(1, gray(1 + i))
+
+    @pl.loop(14, 17)
+    def _(i):
+        attend(i, False)
 
     out_weights.wait()
     late_at = jnp.clip(late_steps - 9, 0, 7)

time: 74 us -> 71.9 us (0.972)
  Pallas kernels: 72 us -> 69.8 us
    pallas_call x1, Pallas kernels: 69.9 us -> 67.7 us  [shards(): pl.pallas_call(kernel, out_shape=(jax.ShapeDtypeStruct(q_nope.shape, BF16...]
where the time goes in v5:
time: 71.9 us; the launch traced here: 70.5 us
  Pallas kernels  69.8 us (97%)
    pallas_call x1, Pallas kernels, shards(): pl.pallas_call(kernel, out_shape=(jax.ShapeDtypeStruct(q_nope.shape, BF16...  67.7 us
    pallas_call x1, Pallas kernels, shards(): pl.pallas_call(hand_over, out_shape=tuple((jax.ShapeDtypeStruct(r.shape,...  2.15 us

profile of v5, /device:TPU:1, one launch (start us, length us, event | category | flops | bytes accessed | tf_op | source)
XLA Modules:
  0.0 70.5 jit_solution(1695035210623948119)
XLA Ops:
  0.6 67.7 %attend_and_dispatch.1 = (bf16[128,2048]{1,0:T(8,128)(2,1)}, bf16[128,1792]{1,0:T(8,128)(2,1)}) custom-call(s32[32,128]{1,0:T(8,128)} %bitcast.4, bf16[128,512]{1,0:T(8,128)(2,1)} %latent_h.1, bf16[64,128]{1,0:T(8,128)(2,1)} %bitcast.5, bf16[128,1792]{1,0:T(8,128)(2,1)} %rows_h.1, s32[8,128]{1,0:T(8,128)} %bitcast.6, f32[8,128]{1,0:T(8,128)} %bitcast.7, ...), custom_call_target="tpu_custom_call" | custom-call | tf_op jit(solution)/shard_map/attend_and_dispatch/pallas_call | solution.py:658
  68.3 2.2 %hand_over.1 = (bf16[128,2048]{1,0:T(8,128)(2,1)}, bf16[128,1792]{1,0:T(8,128)(2,1)}) custom-call(bf16[128,2048]{1,0:T(8,128)(2,1)} %get-tuple-element.4.attn, bf16[128,1792]{1,0:T(8,128)(2,1)} %get-tuple-element.5.moe), custom_call_target="tpu_custom_call" | custom-call | tf_op jit(solution)/shard_map/hand_over/pallas_call | solution.py:732
